TPU v7x, 32 devices: a whole 2x2x4 slice. The times are simulated.
32 devices in a mesh: dev: 8 (over y, x, core), ha: 4 (over z).
Axes of the slice: x: 2, y: 2, z: 4, core: 2. Of those that a mesh axis runs over, the one named last changes fastest.
Arguments:
- volume: bfloat16 [4, 64, 64, 512], P(None, 'dev', 'ha'), may hold values from -6 to 6
- w_first: bfloat16 [3, 3, 3, 4, 32], replicated, may hold values from -0.625 to 0.625
- w_second: bfloat16 [3, 3, 3, 32, 64], replicated, may hold values from -0.21875 to 0.21875
- w_third: bfloat16 [3, 3, 3, 64, 128], P(None, None, None, None, 'ha'), may hold values from -0.15625 to 0.15625
- cotangent: bfloat16 [128, 8, 8, 64], P('ha', 'dev'), may hold values from -6 to 6
Outputs:
- out_third: bfloat16 [128, 8, 8, 64], P('ha', 'dev')
- grad_first: float32 [3, 3, 3, 4, 32], replicated
- grad_second: float32 [3, 3, 3, 32, 64], replicated
- grad_third: float32 [3, 3, 3, 64, 128], P(None, None, None, None, 'ha')
All inputs are finite; a program needn't handle non-finite values.
Results may differ from a plain program's by a relative error of at most 0.0063.
Values may be sent and summed in bfloat16 or wider, within the bound.
No kernel may reach another device: no remote copies, remote signals or barrier semaphores. Data moves between devices by JAX's collectives and lax.ppermute only.
A program may use at most 192 MiB of HBM per device.

v0:
```python
import math

import jax
import jax.numpy as jnp
import numpy as np
from jax import lax
from jax.experimental import pallas as pl
from jax.experimental.pallas import tpu as pltpu
from jax.sharding import PartitionSpec as P

BF = jnp.bfloat16
F32 = jnp.float32
PARAMS = pltpu.CompilerParams(vmem_limit_bytes=48 * 1024 * 1024)


def shifted(block, axis, distance):
    devices = range(lax.axis_size(axis))
    route = [(i - distance, i) for i in devices if i - distance in devices]
    return lax.ppermute(block, axis, route)


def mm(left, right):
    return jnp.dot(left, right, preferred_element_type=F32)


def mm_nt(left, right):
    return lax.dot_general(left, right, (((1,), (1,)), ((), ())), preferred_element_type=F32)


def leaky_and_slope(z):
    u = 4.0 * z
    t = jnp.exp(-jnp.abs(u))
    s = 1.0 + t
    act = 0.3 * z + 0.175 * (jnp.maximum(u, 0.0) + jnp.log(s))
    r = 1.0 / s
    slope = 0.3 + 0.7 * jnp.where(u >= 0.0, r, t * r)
    return act, slope


def row_height(r):
    return np.where(r < 64, r % 16, (r - 64) % 8 - 8)


def row_channel(r):
    return np.where(r < 64, r // 16, (r - 64) // 8)


def constants(width):
    s = width // 8
    sel = np.zeros((width, 3 * 4 * s), np.float32)
    for e in range(3):
        for k, t in enumerate((0, 2, 1, 3)):
            for c in range(s):
                w = 8 * c + 2 * t - 1 + e
                if w >= 0:
                    sel[w, e * 4 * s + k * s + c] = 1
    cols = np.arange(288)
    a, r = cols // 96, cols % 96
    am = a * 4 + row_channel(r)
    h = row_height(r)
    rows = np.arange(352)
    j = rows // 32 - 3
    spread_o = (rows[:, None] % 32 == np.arange(32)[None]).astype(np.float32)
    spread_am = (np.arange(16)[:, None] == am[None]).astype(np.float32)
    mask = np.stack([(h[None] == (2 * j - 1 + b)[:, None]) for b in range(3)]).astype(np.float32)
    later = np.zeros((2 * s, 2 * s), np.float32)
    for c in range(s):
        later[c, s + c] = 1
        if c + 1 < s:
            later[s + c, c + 1] = 1
    pair = np.zeros((4 * s, 6 * s), np.float32)
    for k in range(2):
        for c in range(s):
            pair[k * 2 * s + c, 2 * s + k * s + c] = 1
            pair[k * 2 * s + s + c, 4 * s + k * s + c] = 1
            if c + 1 < s:
                pair[k * 2 * s + s + c, k * s + c + 1] = 1
    spread = np.zeros((2 * s, 12 * s), np.float32)
    for k in range(2):
        for c in range(s):
            base = k * 6 * s
            spread[k * s + c, base + c] = 1
            spread[k * s + c, base + 2 * s + s + c] = 1
            if c > 0:
                spread[k * s + c, base + 4 * s + s + c - 1] = 1
    return {
        "sel": sel, "spread_o": spread_o, "spread_am": spread_am, "mask": mask,
        "later": later, "pair": pair, "spread": spread,
    }


def prep_kernel(own_ref, sel_ref, wbe_ref, so_ref, sam_ref, mask_ref, x_ref, t_ref):
    x_ref[...] = mm(own_ref[...], sel_ref[...]).astype(BF)
    for e in range(3):
        total = None
        for b in range(3):
            rows = mm(so_ref[...], wbe_ref[b * 3 + e]).astype(BF)
            term = mm(rows, sam_ref[...]) * mask_ref[b].astype(F32)
            total = term if total is None else total + term
        t_ref[e] = total.astype(BF)


def forward_kernel(
    xown_ref, hz_ref, dd_ref, sel_ref, t_ref, w2t_ref, w3t_ref, cot_ref, later_ref, pair_ref,
    out_ref, d3_ref, g3_ref, sz_ref, sd_ref, x1_ref, a1_ref, slope1_ref, slope2_ref, a2_ref,
):
    low_dev = (lax.axis_index("dev") > 0).astype(F32)
    low_ha = (lax.axis_index("ha") > 0).astype(F32)
    x1_ref[0:672] = mm(dd_ref[...], sel_ref[...]).astype(BF)
    hz = mm(hz_ref[...], sel_ref[...]).astype(BF)
    for d in range(8):
        base = (7 + d) * 96
        x1_ref[base:base + 64] = xown_ref[d * 64:d * 64 + 64]
        x1_ref[base + 64:base + 96] = hz[d * 32:d * 32 + 32]
    for ii in range(7):
        lo = ii * 192
        z = None
        for e in range(3):
            term = mm(t_ref[e], x1_ref[lo:lo + 288, e * 256:e * 256 + 256])
            z = term if z is None else z + term
        act, slope = leaky_and_slope(z)
        rows = lax.broadcasted_iota(jnp.int32, act.shape, 0)
        keep = jnp.where(rows < 96, low_ha, 1.0)
        if ii < 3:
            keep = keep * low_dev
        act = (act * keep).astype(BF)
        a1_ref[ii, :, 128:384] = act
        a1_ref[ii, :, 0:128] = mm(act[:, 128:256], later_ref[...]).astype(BF)
        if ii >= 3:
            slope1_ref[ii - 3] = slope[96:352]

    def patch(p, q):
        return jnp.concatenate(
            [
                a1_ref[2 * p + 2 + a, (2 * q + 2 + b) * 32:(2 * q + 3 + b) * 32, e * 128:e * 128 + 128]
                for a in range(3) for b in range(3) for e in range(3)
            ], 0)

    w2t = w2t_ref[...]
    for p in range(-1, 2):
        for group in ((-1, 0), (1, 2), (3,)):
            x = jnp.concatenate([patch(p, q) for q in group], 1)
            act, slope = leaky_and_slope(mm(w2t, x))
            for k, q in enumerate(group):
                part = act[:, k * 128:k * 128 + 128]
                if p < 0:
                    part = part * low_dev
                if q < 0:
                    part = part * low_ha
                a2_ref[p + 1, (q + 1) * 64:(q + 2) * 64] = part.astype(BF)
                if p >= 0 and q >= 0:
                    slope2_ref[p, q * 64:q * 64 + 64] = slope[:, k * 128:k * 128 + 128]
    pieces = []
    for a in range(3):
        both = jnp.concatenate([a2_ref[a, 0:192], a2_ref[a, 128:320]], 1)
        spread = mm(both, pair_ref[...]).astype(BF)
        for b in range(3):
            for e in range(3):
                pieces.append(spread[b * 64:b * 64 + 64, e * 128:e * 128 + 128])
    x3 = jnp.concatenate(pieces, 0)
    act, slope = leaky_and_slope(mm(w3t_ref[...], x3))
    out_ref[...] = act.astype(BF)
    d3 = (cot_ref[...].astype(F32) * slope).astype(BF)
    d3_ref[...] = d3
    g3 = mm_nt(d3, x3).astype(BF)
    parts, _, lanes = g3_ref.shape
    for c in range(parts):
        have = min(max(1728 - c * lanes, 0), lanes)
        if have == lanes:
            g3_ref[c] = g3[:, c * lanes:(c + 1) * lanes]
        else:
            g3_ref[c] = jnp.zeros((128, lanes), BF)
            if have > 0:
                g3_ref[c, :, 0:have] = g3[:, c * lanes:c * lanes + have]
    sz_ref[0:128] = d3
    sd_ref[0:128] = d3
    for p in range(2):
        sz_ref[128 + 64 * p:192 + 64 * p] = slope2_ref[p, 0:64].astype(BF)
    sd_ref[128:384] = slope2_ref[0].astype(BF)


def backward_kernel(
    d3_ref, rz_ref, rd_ref, x1_ref, a1_ref, slope1_ref, slope2_ref, w3g_ref, w2e_ref, w2o_ref,
    later_ref, spread_ref, so_ref, sam_ref, mask_ref,
    msg_ref, d2_ref, d1_ref,
):
    spread = spread_ref[...]

    def blocks(pair, last):
        both = mm(pair, spread).astype(BF)
        lone = mm(last, spread[:, 0:384]).astype(BF)
        cols = [both[:, 0:384], both[:, 384:768], lone]
        return jnp.concatenate(
            [jnp.concatenate([c[:, e * 128:e * 128 + 128] for e in range(3)], 0) for c in cols], 1)

    u0 = mm(w3g_ref[192:576], blocks(d3_ref[...], rz_ref[0:128]))
    u1 = mm(w3g_ref[0:384], blocks(rd_ref[0:128], rd_ref[384:512]))
    u = {(0, 1): u0[0:192], (0, 2): u0[192:384], (1, 0): u1[0:192], (1, 1): u1[192:384]}
    taps = {0: ((1, 0),), 1: ((2, 0), (0, 1)), 2: ((1, 1),), 3: ((2, 1), (0, 2)), 4: ((1, 2),)}
    for x in range(3):
        for y in range(5):
            back = None
            for a, i in taps[x]:
                for b, j in taps[y]:
                    term = u[(i, a)][b * 64:b * 64 + 64, j * 128:j * 128 + 128]
                    back = term if back is None else back + term
            if x < 2 and y < 4:
                slope = slope2_ref[x, y * 64:y * 64 + 64]
            elif x < 2:
                slope = rz_ref[128 + 64 * x:192 + 64 * x].astype(F32)
            elif y < 4:
                slope = rd_ref[128 + 64 * y:192 + 64 * y].astype(F32)
            else:
                slope = rd_ref[512:576].astype(F32)
            d2_ref[x, :, y * 128:y * 128 + 128] = (back * slope).astype(BF)

    def patch(p, q):
        return jnp.concatenate(
            [
                a1_ref[2 * p + 2 + a, (2 * q + 2 + b) * 32:(2 * q + 3 + b) * 32, e * 128:e * 128 + 128]
                for a in range(3) for b in range(3) for e in range(3)
            ], 0)

    g2 = None
    for p in range(2):
        for q in (0, 2):
            x = jnp.concatenate([patch(p, q), patch(p, q + 1)], 1)
            term = mm_nt(x, d2_ref[p, :, q * 128:q * 128 + 256])
            g2 = term if g2 is None else g2 + term
    msg_ref[0:432] = jnp.concatenate([g2[0:432], g2[432:864]], 1).astype(BF)

    ue, uo = {}, {}
    for p, first, end in ((0, 1, 3), (1, 0, 3), (2, 0, 1)):
        d2 = d2_ref[p]
        moved = jnp.concatenate(
            [mm_nt(d2[:, q * 128:q * 128 + 128], later_ref[...]).astype(BF) for q in range(5)], 1)
        e_part = mm(w2e_ref[first * 96:end * 96], d2)
        o_part = mm(w2o_ref[first * 96:end * 96], jnp.concatenate([d2, moved], 0))
        for a in range(first, end):
            lo = (a - first) * 96
            ue[(p, a)] = e_part[lo:lo + 96]
            uo[(p, a)] = o_part[lo:lo + 96]
    for x in range(4):
        for y in range(8):
            if y % 2 == 0:
                y_taps = ((1, y // 2),)
            else:
                y_taps = ((2, y // 2), (0, y // 2 + 1))
            x_taps = ((1, x // 2),) if x % 2 == 0 else ((2, x // 2), (0, x // 2 + 1))
            for k, source in ((0, ue), (1, uo)):
                back = None
                for a, p in x_taps:
                    for b, q in y_taps:
                        term = source[(p, a)][b * 32:b * 32 + 32, q * 128:q * 128 + 128]
                        back = term if back is None else back + term
                slope = slope1_ref[x, y * 32:y * 32 + 32, k * 128:k * 128 + 128]
                d1_ref[y * 32:y * 32 + 32, x * 256 + k * 128:x * 256 + k * 128 + 128] = (back * slope).astype(BF)

    d1 = d1_ref[...]
    so = so_ref[0:256]
    sam = sam_ref[...]
    columns = []
    grads = []
    for e in range(3):
        x = jnp.concatenate([x1_ref[(2 * i + 6) * 96:(2 * i + 6) * 96 + 288, e * 256:e * 256 + 256] for i in range(4)], 1)
        grads.append(mm_nt(x, d1))
    for b in range(3):
        for e in range(3):
            kept = grads[e] * mask_ref[b].astype(F32)
            high = kept.astype(BF)
            low = (kept - high.astype(F32)).astype(BF)
            columns.append(mm(high, so) + mm(low, so))
    wide = jnp.concatenate(columns, 1)
    high = wide.astype(BF)
    low = (wide - high.astype(F32)).astype(BF)
    g1 = (mm(sam, high) + mm(sam, low)).astype(BF)
    msg_ref[432:512] = jnp.zeros((80, 128), BF)
    msg_ref[432:448] = g1[:, 0:128]
    msg_ref[448:464] = g1[:, 128:256]
    msg_ref[464:480, 0:32] = g1[:, 256:288]


def local(volume, w_first, w_second, w_third, cotangent):
    nd, nh = lax.axis_size("dev"), lax.axis_size("ha")
    depth_total = volume.shape[1] * nd
    height_total = volume.shape[2] * nh
    width = volume.shape[3]
    cells = depth_total * height_total * width
    scale_first, scale_second, scale_third = (1.0 / math.sqrt(cells // 8 ** k) for k in (1, 2, 3))
    const = {k: jnp.asarray(v, BF) for k, v in constants(width).items()}
    vmem = pltpu.VMEM

    hz = shifted(volume[:, :, 8:].transpose(1, 0, 2, 3).reshape(8, 32, width), "ha", 1)
    own = volume.transpose(1, 0, 2, 3).reshape(8, 64, width)
    dd = shifted(jnp.concatenate([own[1:], hz[1:]], 1), "dev", 1)

    w3t = lax.all_gather(w_third.reshape(1728, -1).T, "ha", axis=0, tiled=True)
    share = cotangent[:, 0].reshape(-1, nh, 2, 64).transpose(1, 0, 2, 3)
    cot = lax.all_to_all(share, "ha", 0, 0, tiled=True)
    cot = cot.reshape(128, 128)
    w2t = w_second.reshape(864, 64).T
    wbe = w_first.transpose(1, 2, 4, 0, 3).reshape(9, 32, 12)
    wbe = jnp.pad(wbe, ((0, 0), (0, 0), (0, 4)))

    xown, t1 = pl.pallas_call(
        prep_kernel,
        out_shape=(jax.ShapeDtypeStruct((512, 768), BF), jax.ShapeDtypeStruct((3, 352, 288), BF)),
        compiler_params=PARAMS,
        cost_estimate=pl.CostEstimate(flops=1 << 29, bytes_accessed=1 << 22, transcendentals=0),
        name="prep",
    )(own.reshape(512, width), const["sel"], wbe, const["spread_o"], const["spread_am"], const["mask"])

    out3, d3, g3, sz, sd, x1, a1, slope1, slope2 = pl.pallas_call(
        forward_kernel,
        out_shape=(
            jax.ShapeDtypeStruct((128, 128), BF),
            jax.ShapeDtypeStruct((128, 128), BF),
            jax.ShapeDtypeStruct((nd, 128, 2048 // nd), BF),
            jax.ShapeDtypeStruct((256, 128), BF),
            jax.ShapeDtypeStruct((384, 128), BF),
            jax.ShapeDtypeStruct((1440, 768), BF),
            jax.ShapeDtypeStruct((7, 352, 384), BF),
            jax.ShapeDtypeStruct((4, 256, 256), F32),
            jax.ShapeDtypeStruct((2, 256, 128), F32),
        ),
        scratch_shapes=[vmem((3, 320, 128), BF)],
        compiler_params=PARAMS,
        cost_estimate=pl.CostEstimate(flops=1 << 32, bytes_accessed=1 << 23, transcendentals=1 << 21),
        name="forward",
    )(xown, hz.reshape(256, width), dd.reshape(672, width), const["sel"], t1, w2t, w3t, cot, const["later"], const["pair"])

    rz = shifted(sz, "ha", -1)
    rd = shifted(jnp.concatenate([sd, rz[0:192]], 0), "dev", -1)

    sent = g3.reshape(nd * nh, 128 // nh, 2048 // nd)
    parts = lax.all_to_all(sent, ("dev", "ha"), 0, 0, tiled=True)
    chunk = jnp.sum(parts.astype(F32), 0) * scale_third
    everything = lax.all_gather(chunk, "dev", axis=0)
    grad_third = everything.transpose(1, 0, 2).reshape(128 // nh, 2048)[:, :1728]
    grad_third = grad_third.T.reshape(3, 3, 3, 64, 128 // nh)
    share = lax.all_to_all(out3.reshape(nh, 128 // nh, 128), "ha", 0, 0, tiled=True)
    out_third = share.reshape(nh, 128 // nh, 2, 64).transpose(1, 0, 2, 3).reshape(128 // nh, 1, 2 * nh, 64)

    order = jnp.array([1, 2, 0])
    w3g = w3t.reshape(128, 9, 3, 64).transpose(1, 3, 2, 0)
    w3g = jnp.concatenate([w3g[:, :, 1], w3g[:, :, 2], w3g[:, :, 0]], 2).reshape(576, 384)
    taps = w_second.reshape(9, 3, 32, 64)
    w2e = taps[:, 1].reshape(288, 64)
    w2o = jnp.concatenate([taps[:, 2], taps[:, 0]], 2).reshape(288, 128)
    mask_own = const["mask"][:, 96:].transpose(0, 2, 1)
    msg = pl.pallas_call(
        backward_kernel,
        out_shape=jax.ShapeDtypeStruct((512, 128), BF),
        scratch_shapes=[vmem((3, 64, 640), BF), vmem((256, 1024), BF)],
        compiler_params=PARAMS,
        cost_estimate=pl.CostEstimate(flops=1 << 32, bytes_accessed=1 << 23, transcendentals=0),
        name="backward",
    )(d3, rz, rd, x1, a1, slope1, slope2, w3g, w2e, w2o, const["later"], const["spread"],
      const["spread_o"], const["spread_am"], mask_own)

    n = nd * nh
    parts = lax.all_to_all(msg.reshape(n, 512 // n, 128), ("dev", "ha"), 0, 0, tiled=True)
    chunk = jnp.sum(parts.astype(F32), 0).astype(BF)
    spread = jnp.broadcast_to(chunk[None], (n, 512 // n, 128))
    total = lax.all_to_all(spread, ("dev", "ha"), 0, 0, tiled=True).reshape(512, 128).astype(F32)
    grad_second = jnp.concatenate([total[0:432, 0:64], total[0:432, 64:128]], 0) * scale_second
    grad_second = grad_second.reshape(3, 3, 3, 32, 64)
    flat = jnp.concatenate([total[432:444], total[448:460], total[464:476, 0:32]], 1) * scale_first
    grad_first = flat.reshape(3, 4, 3, 3, 32).transpose(0, 2, 3, 1, 4)
    return out_third, grad_first, grad_second, grad_third


def solution(mesh):
    placed = (
        P(None, "dev", "ha", None),
        P(),
        P(),
        P(None, None, None, None, "ha"),
        P("ha", "dev", None, None),
    )
    return jax.shard_map(
        local,
        mesh=mesh,
        in_specs=placed,
        out_specs=(P("ha", "dev", None, None), P(), P(), P(None, None, None, None, "ha")),
        check_vma=False,
    )
```

profile of v0, /device:TPU:0, one launch (start us, length us, event | category | flops | bytes accessed | tf_op | source)
XLA Modules:
  0.0 136.4 jit_solution(14616465747618563282)
XLA Ops:
  0.6 1.1 copy.63
  1.7 4.9 %collective-permute-start = (bf16[8,32,512]{2,1,0:T(8,128)(2,1)S(1)}, bf16[8,32,512]{2,1,0:T(8,128)(2,1)S(1)}, u32[]{:S(2)}, u32[]{:S(2)}) collective-permute-start(bf16[8,32,512]{2,1,0:T(8,128)(2,1)S(1)} %slice_bitcast_fusion), channel_id=1, source_target_pairs={{0,1},{1,2},{2,3},{4,5},{5,6},{6,7},{8,9},{9,10},{10,11},{12,13},{... | collective-permute-start | bytes 786440 | tf_op jit(solution)/shard_map/ppermute | solution.py:19
  6.8 5.5 %collective-permute-done = bf16[8,32,512]{2,1,0:T(8,128)(2,1)S(1)} collective-permute-done((bf16[8,32,512]{2,1,0:T(8,128)(2,1)S(1)}, bf16[8,32,512]{2,1,0:T(8,128)(2,1)S(1)}, u32[]{:S(2)}, u32[]{:S(2)}) %collective-permute-start) | collective-permute-done | bytes 262176 | tf_op jit(solution)/shard_map/ppermute | solution.py:19
  12.3 0.9 pad_maximum_fusion
  13.2 2.1 %collective-permute-start.1 = (bf16[7,96,512]{2,1,0:T(8,128)(2,1)}, bf16[7,96,512]{2,1,0:T(8,128)(2,1)}, u32[]{:S(2)}, u32[]{:S(2)}) collective-permute-start(bf16[7,96,512]{2,1,0:T(8,128)(2,1)} %pad_maximum_fusion), channel_id=1, source_target_pairs={{0,4},{4,8},{8,12},{12,16},{16,20},{20,24},{24,28},{1,5},{5,9},{9,... | collective-permute-start | bytes 2064392 | tf_op jit(solution)/shard_map/ppermute | solution.py:19
  15.4 0.7 reshape.109
  16.1 5.8 %all-to-all-start = ((bf16[4,2,2048]{2,1,0:T(2,128)(2,1)}), bf16[4,2,2048]{2,1,0:T(2,128)(2,1)S(1)}, u32[]{:S(2)}, u32[]{:S(2)}) async-start(bf16[4,2,2048]{2,1,0:T(2,128)(2,1)} %reshape.109), calls=%async_computation | async-start | bytes 65536 | tf_op jit(solution)/shard_map/all_to_all | solution.py:299
  21.9 0.8 copy.42
  23.3 16.4 %all_gather.7.w3t_ref = bf16[128,1728]{1,0:T(8,128)(2,1)S(1)} all-gather(bf16[32,1728]{1,0:T(8,128)(2,1)S(1)} %bitcast.75), channel_id=1, replica_groups=mesh['dev'=8,'ha'=4] {'ha'}, dimensions={0}, use_global_device_ids=true | all-gather | bytes 552960 | tf_op jit(solution)/shard_map/all_gather | solution.py:297
  40.0 0.9 pad.4.wbe_ref
  40.9 0.8 fusion
  41.7 2.5 %prep.1 = (bf16[512,768]{1,0:T(8,128)(2,1)S(1)}, bf16[3,352,288]{2,1,0:T(8,128)(2,1)S(1)}) custom-call(bf16[512,512]{1,0:T(8,128)(2,1)S(1)} %bitcast.61, bf16[512,768]{1,0:T(8,128)(2,1)S(1)} %copy-done.1, bf16[9,32,16]{2,1,0:T(8,128)(2,1)S(1)} %pad.4.wbe_ref, bf16[352,32]{1,0:T(8,128)(2,1)S(1)} %copy-done.2, bf16[16,288]{1,0:T(8,128)(2,1)S(1)} %copy-done.3, ...), custom_call_target="tpu_custom_call" | custom-call | flops 536870912 | bytes 4194304 | tf_op jit(solution)/shard_map/prep/pallas_call | solution.py:305
  44.2 0.9 copy-done.4
  45.1 0.9 copy-done.6
  46.3 1.1 copy-done.5
  47.4 1.1 copy-done.7
  48.6 11.5 %forward.1 = (bf16[128,128]{1,0:T(8,128)(2,1)}, bf16[128,128]{1,0:T(8,128)(2,1)S(1)}, bf16[8,128,256]{2,1,0:T(8,128)(2,1)}, bf16[256,128]{1,0:T(8,128)(2,1)S(1)}...) custom-call(bf16[512,768]{1,0:T(8,128)(2,1)S(1)} %copy-done.7, ...), custom_call_target="tpu_custom_call" | custom-call | flops 4294967296 | bytes 8388608 | tf_op jit(solution)/shard_map/forward/pallas_call | solution.py:313
  60.0 1.4 %collective-permute-start.2 = (bf16[256,128]{1,0:T(8,128)(2,1)S(1)}, bf16[256,128]{1,0:T(8,128)(2,1)S(1)}, u32[]{:S(2)}, u32[]{:S(2)}) collective-permute-start(bf16[256,128]{1,0:T(8,128)(2,1)S(1)} %get-tuple-element.19), channel_id=1, source_target_pairs={{1,0},{2,1},{3,2},{5,4},{6,5},{7,6},{9,8},{10,9},{11,10},{13,12},{... | collective-permute-start | bytes 196616 | tf_op jit(solution)/shard_map/ppermute | solution.py:19
  61.5 4.8 %collective-permute-done.2.rz_ref = bf16[256,128]{1,0:T(8,128)(2,1)S(1)} collective-permute-done((bf16[256,128]{1,0:T(8,128)(2,1)S(1)}, bf16[256,128]{1,0:T(8,128)(2,1)S(1)}, u32[]{:S(2)}, u32[]{:S(2)}) %collective-permute-start.2) | collective-permute-done | bytes 65568 | tf_op jit(solution)/shard_map/ppermute | solution.py:19
  66.3 1.5 %collective-permute-start.3 = (bf16[576,128]{1,0:T(8,128)(2,1)S(1)}, bf16[576,128]{1,0:T(8,128)(2,1)S(1)}, u32[]{:S(2)}, u32[]{:S(2)}) collective-permute-start(bf16[576,128]{1,0:T(8,128)(2,1)S(1)} %pad_maximum_fusion.2), channel_id=1, source_target_pairs={{4,0},{8,4},{12,8},{16,12},{20,16},{24,20},{28,24},{5,1},{9,5},{13... | collective-permute-start | bytes 442376 | tf_op jit(solution)/shard_map/ppermute | solution.py:19
  68.0 1.6 %collective-permute-done.3.rd_ref = bf16[576,128]{1,0:T(8,128)(2,1)S(1)} collective-permute-done((bf16[576,128]{1,0:T(8,128)(2,1)S(1)}, bf16[576,128]{1,0:T(8,128)(2,1)S(1)}, u32[]{:S(2)}, u32[]{:S(2)}) %collective-permute-start.3) | collective-permute-done | bytes 147488 | tf_op jit(solution)/shard_map/ppermute | solution.py:19
  69.6 1.5 %copy-done.12 = bf16[7,352,384]{2,1,0:T(8,128)(2,1)S(1)} copy-done((bf16[7,352,384]{2,1,0:T(8,128)(2,1)S(1)}, bf16[7,352,384]{2,1,0:T(8,128)(2,1)}, u32[]{:S(2)}) %copy-start.12) | copy-done | bytes 1892376
  71.1 5.3 %backward.1 = bf16[512,128]{1,0:T(8,128)(2,1)S(1)} custom-call(bf16[128,128]{1,0:T(8,128)(2,1)S(1)} %get-tuple-element.18.d3_ref, bf16[256,128]{1,0:T(8,128)(2,1)S(1)} %collective-permute-done.2.rz_ref, bf16[576,128]{1,0:T(8,128)(2,1)S(1)} %collective-permute-done.3.rd_ref, bf16[1440,768]{1,0:T(8,128)(2,1)} %get-tuple-element.21.x1_ref, ...), custom_call_target="tpu_custom_call" | custom-call | flops 4294967296 | bytes 8388608 | tf_op jit(solution)/shard_map/backward/pallas_call | solution.py:351
  76.4 13.5 %all_to_all.25 = bf16[32,16,128]{2,1,0:T(8,128)(2,1)S(1)} all-to-all(bf16[32,16,128]{2,1,0:T(8,128)(2,1)S(1)} %bitcast.63), channel_id=1, replica_groups=mesh['dev'=8,'ha'=4] {'dev','ha'}, dimensions={0} | all-to-all | bytes 262144 | tf_op jit(solution)/shard_map/all_to_all | solution.py:362
  89.9 3.3 %all-to-all-start.1 = ((bf16[4,32,128]{2,1,0:T(8,128)(2,1)}), bf16[4,32,128]{2,1,0:T(8,128)(2,1)S(1)}, u32[]{:S(2)}, u32[]{:S(2)}) async-start(bf16[4,32,128]{2,1,0:T(8,128)(2,1)} %bitcast.13), calls=%async_computation.1 | async-start | bytes 65536 | tf_op jit(solution)/shard_map/all_to_all | solution.py:341
  93.2 5.6 %all-to-all-done.1 = bf16[4,32,128]{2,1,0:T(8,128)(2,1)S(1)} async-done(((bf16[4,32,128]{2,1,0:T(8,128)(2,1)}), bf16[4,32,128]{2,1,0:T(8,128)(2,1)S(1)}, u32[]{:S(2)}, u32[]{:S(2)}) %all-to-all-start.1) | async-done | bytes 32800 | tf_op jit(solution)/shard_map/all_to_all | solution.py:341
  98.8 10.1 %all_to_all.26 = bf16[32,16,128]{2,1,0:T(8,128)(2,1)S(1)} all-to-all(bf16[32,16,128]{2,1,0:T(8,128)(2,1)S(1)} %broadcast_in_dim.2), channel_id=1, replica_groups=mesh['dev'=8,'ha'=4] {'dev','ha'}, dimensions={0} | all-to-all | bytes 262144 | tf_op jit(solution)/shard_map/all_to_all | solution.py:365
  108.9 2.6 %all-to-all-start.4 = ((bf16[32,32,256]{2,1,0:T(8,128)(2,1)}), bf16[32,32,256]{2,1,0:T(8,128)(2,1)S(1)}, u32[]{:S(2)}, u32[]{:S(2)}) async-start(bf16[32,32,256]{2,1,0:T(8,128)(2,1)} %bitcast.31), calls=%async_computation.4 | async-start | bytes 1048576 | tf_op jit(solution)/shard_map/all_to_all | solution.py:336
  113.2 0.8 maximum_multiply_fusion
  114.0 11.9 %all-to-all-done.4 = bf16[32,32,256]{2,1,0:T(8,128)(2,1)S(1)} async-done(((bf16[32,32,256]{2,1,0:T(8,128)(2,1)}), bf16[32,32,256]{2,1,0:T(8,128)(2,1)S(1)}, u32[]{:S(2)}, u32[]{:S(2)}) %all-to-all-start.4) | async-done | bytes 524320 | tf_op jit(solution)/shard_map/all_to_all | solution.py:336
  126.0 9.3 %all-gather = f32[256,256]{1,0:T(8,128)S(1)} all-gather(f32[32,256]{1,0:T(8,128)S(1)} %broadcast_multiply_fusion), channel_id=2, replica_groups=mesh['dev'=8,'ha'=4] {'dev'}, dimensions={0}, use_global_device_ids=true | all-gather | bytes 294912 | tf_op jit(solution)/shard_map/all_gather | solution.py:338
  135.6 0.8 copy.54
  (74 shorter events, 3.5 us)
Async XLA Ops:
  1.7 10.5 %collective-permute-start = (bf16[8,32,512]{2,1,0:T(8,128)(2,1)S(1)}, bf16[8,32,512]{2,1,0:T(8,128)(2,1)S(1)}, u32[]{:S(2)}, u32[]{:S(2)}) collective-permute-start(bf16[8,32,512]{2,1,0:T(8,128)(2,1)S(1)} %slice_bitcast_fusion), channel_id=1, source_target_pairs={{0,1},{1,2},{2,3},{4,5},{5,6},{6,7},{8,9},{9,10},{10,11},{12,13},{... | collective-permute-start | bytes 786440 | tf_op jit(solution)/shard_map/ppermute | solution.py:19
  6.7 8.6 %copy-start.20 = (bf16[32,1,8,64]{3,2,1,0:T(8,128)(2,1)S(1)}, bf16[32,1,8,64]{3,2,1,0:T(8,128)(2,1)}, u32[]{:S(2)}) copy-start(bf16[32,1,8,64]{3,2,1,0:T(8,128)(2,1)} %param.16) | copy-start | bytes 98308
  6.7 15.2 %copy-start.21 = (bf16[3,3,3,4,32]{4,3,2,1,0:T(4,128)(2,1)S(1)}, bf16[3,3,3,4,32]{4,3,2,1,0:T(4,128)(2,1)}, u32[]{:S(2)}) copy-start(bf16[3,3,3,4,32]{4,3,2,1,0:T(4,128)(2,1)} %param.13) | copy-start | bytes 20740
  6.8 16.0 %copy-start.19 = (bf16[3,3,3,64,32]{3,4,2,1,0:T(8,128)(2,1)S(1)}, bf16[3,3,3,64,32]{3,4,2,1,0:T(8,128)(2,1)}, u32[]{:S(2)}) copy-start(bf16[3,3,3,64,32]{3,4,2,1,0:T(8,128)(2,1)} %param.15) | copy-start | bytes 331780
  12.2 10.8 %copy-start.14 = (bf16[3,3,3,32,64]{4,3,2,1,0:T(8,128)(2,1)S(1)}, bf16[3,3,3,32,64]{4,3,2,1,0:T(8,128)(2,1)}, u32[]{:S(2)}) copy-start(bf16[3,3,3,32,64]{4,3,2,1,0:T(8,128)(2,1)} %param.14) | copy-start | bytes 331780
  13.2 33.1 %collective-permute-start.1 = (bf16[7,96,512]{2,1,0:T(8,128)(2,1)}, bf16[7,96,512]{2,1,0:T(8,128)(2,1)}, u32[]{:S(2)}, u32[]{:S(2)}) collective-permute-start(bf16[7,96,512]{2,1,0:T(8,128)(2,1)} %pad_maximum_fusion), channel_id=1, source_target_pairs={{0,4},{4,8},{8,12},{12,16},{16,20},{20,24},{24,28},{1,5},{5,9},{9,... | collective-permute-start | bytes 2064392 | tf_op jit(solution)/shard_map/ppermute | solution.py:19
  16.1 29.9 %all-to-all-start = ((bf16[4,2,2048]{2,1,0:T(2,128)(2,1)}), bf16[4,2,2048]{2,1,0:T(2,128)(2,1)S(1)}, u32[]{:S(2)}, u32[]{:S(2)}) async-start(bf16[4,2,2048]{2,1,0:T(2,128)(2,1)} %reshape.109), calls=%async_computation | async-start | bytes 65536 | tf_op jit(solution)/shard_map/all_to_all | solution.py:299
  23.1 18.6 %copy-start = (bf16[3,352,288]{2,1,0:T(8,128)(2,1)S(1)}, bf16[3,352,288]{2,1,0:T(8,128)(2,1)}, u32[]{:S(2)}) copy-start(bf16[3,352,288]{2,1,0:T(8,128)(2,1)} %constant.29.clone.mask_ref) | copy-start | bytes 1824772
  23.1 18.6 %copy-start.1 = (bf16[512,768]{1,0:T(8,128)(2,1)S(1)}, bf16[512,768]{1,0:T(8,128)(2,1)}, u32[]{:S(2)}) copy-start(bf16[512,768]{1,0:T(8,128)(2,1)} %constant.26.clone.sel_ref) | copy-start | bytes 2359300
  23.1 18.6 %copy-start.2 = (bf16[352,32]{1,0:T(8,128)(2,1)S(1)}, bf16[352,32]{1,0:T(8,128)(2,1)}, u32[]{:S(2)}) copy-start(bf16[352,32]{1,0:T(8,128)(2,1)} %constant.27.clone.so_ref) | copy-start | bytes 67588
  23.1 18.6 %copy-start.3 = (bf16[16,288]{1,0:T(8,128)(2,1)S(1)}, bf16[16,288]{1,0:T(8,128)(2,1)}, u32[]{:S(2)}) copy-start(bf16[16,288]{1,0:T(8,128)(2,1)} %constant.28.clone.sam_ref) | copy-start | bytes 27652
  41.7 4.6 %copy-start.10 = (bf16[256,384]{1,0:T(8,128)(2,1)S(1)}, bf16[256,384]{1,0:T(8,128)(2,1)}, u32[]{:S(2)}) copy-start(bf16[256,384]{1,0:T(8,128)(2,1)} %constant.31.clone.pair_ref) | copy-start | bytes 589828
  41.7 4.6 %copy-start.11 = (bf16[128,128]{1,0:T(8,128)(2,1)S(1)}, bf16[128,128]{1,0:T(8,128)(2,1)}, u32[]{:S(2)}) copy-start(bf16[128,128]{1,0:T(8,128)(2,1)} %constant.30.clone.later_ref) | copy-start | bytes 98308
  44.2 0.9 copy-start.4
  45.1 0.9 copy-start.6
  46.3 1.1 copy-start.5
  47.4 1.1 copy-start.7
  48.6 12.9 %copy-start.15 = (bf16[3,3,3,32,64]{4,3,2,1,0:T(8,128)(2,1)S(1)}, bf16[3,3,3,32,64]{4,3,2,1,0:T(8,128)(2,1)}, u32[]{:S(2)}) copy-start(bf16[3,3,3,32,64]{4,3,2,1,0:T(8,128)(2,1)} %param.14) | copy-start | bytes 331780
  48.6 19.4 %copy-start.16 = (bf16[9,64,1,128]{3,1,2,0:T(8,128)(2,1)S(1)}, bf16[9,64,1,128]{3,1,2,0:T(8,128)(2,1)}, u32[]{:S(2)}) copy-start(bf16[9,64,1,128]{3,1,2,0:T(8,128)(2,1)} %get-tuple-element.36) | copy-start | bytes 442372
  48.6 19.4 %copy-start.17 = (bf16[9,64,1,128]{3,1,2,0:T(8,128)(2,1)S(1)}, bf16[9,64,1,128]{3,1,2,0:T(8,128)(2,1)}, u32[]{:S(2)}) copy-start(bf16[9,64,1,128]{3,1,2,0:T(8,128)(2,1)} %get-tuple-element.37) | copy-start | bytes 442372
  48.6 19.4 %copy-start.18 = (bf16[9,64,1,128]{3,1,2,0:T(8,128)(2,1)S(1)}, bf16[9,64,1,128]{3,1,2,0:T(8,128)(2,1)}, u32[]{:S(2)}) copy-start(bf16[9,64,1,128]{3,1,2,0:T(8,128)(2,1)} %get-tuple-element.38) | copy-start | bytes 442372
  60.0 9.6 %copy-start.8 = (bf16[3,288,256]{2,1,0:T(8,128)(2,1)S(1)}, bf16[3,288,256]{2,1,0:T(8,128)(2,1)}, u32[]{:S(2)}) copy-start(bf16[3,288,256]{2,1,0:T(8,128)(2,1)} %constant.37.mask_ref) | copy-start | bytes 1327108
  60.0 9.6 %copy-start.9 = (bf16[128,768]{1,0:T(8,128)(2,1)S(1)}, bf16[128,768]{1,0:T(8,128)(2,1)}, u32[]{:S(2)}) copy-start(bf16[128,768]{1,0:T(8,128)(2,1)} %constant.32.clone.spread_ref) | copy-start | bytes 589828
  60.0 9.6 %copy-start.13 = (f32[4,256,256]{2,1,0:T(8,128)S(1)}, f32[4,256,256]{2,1,0:T(8,128)}, u32[]{:S(2)}) copy-start(f32[4,256,256]{2,1,0:T(8,128)} %get-tuple-element.23.slope1_ref) | copy-start | bytes 3145732
  60.0 6.3 %collective-permute-start.2 = (bf16[256,128]{1,0:T(8,128)(2,1)S(1)}, bf16[256,128]{1,0:T(8,128)(2,1)S(1)}, u32[]{:S(2)}, u32[]{:S(2)}) collective-permute-start(bf16[256,128]{1,0:T(8,128)(2,1)S(1)} %get-tuple-element.19), channel_id=1, source_target_pairs={{1,0},{2,1},{3,2},{5,4},{6,5},{7,6},{9,8},{10,9},{11,10},{13,12},{... | collective-permute-start | bytes 196616 | tf_op jit(solution)/shard_map/ppermute | solution.py:19
  66.3 3.3 %collective-permute-start.3 = (bf16[576,128]{1,0:T(8,128)(2,1)S(1)}, bf16[576,128]{1,0:T(8,128)(2,1)S(1)}, u32[]{:S(2)}, u32[]{:S(2)}) collective-permute-start(bf16[576,128]{1,0:T(8,128)(2,1)S(1)} %pad_maximum_fusion.2), channel_id=1, source_target_pairs={{4,0},{8,4},{12,8},{16,12},{20,16},{24,20},{28,24},{5,1},{9,5},{13... | collective-permute-start | bytes 442376 | tf_op jit(solution)/shard_map/ppermute | solution.py:19
  69.6 1.5 %copy-start.12 = (bf16[7,352,384]{2,1,0:T(8,128)(2,1)S(1)}, bf16[7,352,384]{2,1,0:T(8,128)(2,1)}, u32[]{:S(2)}) copy-start(bf16[7,352,384]{2,1,0:T(8,128)(2,1)} %get-tuple-element.22.a1_ref) | copy-start | bytes 5677060
  89.9 8.9 %all-to-all-start.1 = ((bf16[4,32,128]{2,1,0:T(8,128)(2,1)}), bf16[4,32,128]{2,1,0:T(8,128)(2,1)S(1)}, u32[]{:S(2)}, u32[]{:S(2)}) async-start(bf16[4,32,128]{2,1,0:T(8,128)(2,1)} %bitcast.13), calls=%async_computation.1 | async-start | bytes 65536 | tf_op jit(solution)/shard_map/all_to_all | solution.py:341
  108.9 17.0 %all-to-all-start.4 = ((bf16[32,32,256]{2,1,0:T(8,128)(2,1)}), bf16[32,32,256]{2,1,0:T(8,128)(2,1)S(1)}, u32[]{:S(2)}, u32[]{:S(2)}) async-start(bf16[32,32,256]{2,1,0:T(8,128)(2,1)} %bitcast.31), calls=%async_computation.4 | async-start | bytes 1048576 | tf_op jit(solution)/shard_map/all_to_all | solution.py:336
where the time goes:
time: 137 us; the launch traced here: 136 us
  blocking collectives  49.3 us (36%)
  waiting for transfers between devices  29.3 us (21%)
  starting transfers between devices  21.6 us (16%)
  Pallas kernels  19.2 us (14%)
  local copies, waits for them, and re-layouts  13.9 us (10%)
  other arithmetic  2.07 us (2%)
    all_gather x1, blocking collectives, local(): w3t = lax.all_gather(w_third.reshape(1728, -1).T, 'ha', axis=0, tiled=True)  16.4 us
    all_to_all x1, blocking collectives, local(): lax.all_to_all(msg.reshape(n, 512 // n, 128), ('dev', 'ha'), 0, 0, tiled=...  13.5 us
    ppermute x4, waiting for transfers between devices, shifted(): return lax.ppermute(block, axis, route)  11.9 us
    all_to_all x1, waiting for transfers between devices, local(): parts = lax.all_to_all(sent, ('dev', 'ha'), 0, 0, tiled=True)  11.9 us
    pallas_call x1, Pallas kernels, local(): pl.pallas_call(forward_kernel, out_shape=(jax.ShapeDtypeStruct((128, 128)...  11.5 us
    all_to_all x1, blocking collectives, local(): lax.all_to_all(spread, ('dev', 'ha'), 0, 0, tiled=True).reshape(512, 128)  10.1 us
    ppermute x4, starting transfers between devices, shifted(): return lax.ppermute(block, axis, route)  9.98 us
    all_gather x1, blocking collectives, local(): everything = lax.all_gather(chunk, 'dev', axis=0)  9.3 us
  transfers between devices with their start and end apart: 7, of which 5 were waited for; matrix products, arithmetic and copies ran while one was open for 5% of the time, Pallas kernels for 2%

commit v1 on v0

v1 whole, which is shorter than its diff:
```python
import functools
import math

import jax
import jax.numpy as jnp
import numpy as np
from jax import lax
from jax.experimental import pallas as pl
from jax.experimental.pallas import tpu as pltpu
from jax.sharding import PartitionSpec as P

BF = jnp.bfloat16
F32 = jnp.float32
PARK = {"x1": (0, 2592), "a1": (2592, 1760), "x3": (4352, 1728), "slope1": (0, 1024), "slope2": (1024, 512)}
PARK_SHAPES = ((90112, 384), (67584, 256))


def parked(park, name, lanes):
    first, count = PARK[name]
    return park.at[first:first + count, 0:lanes]


def call(name, body, inputs, far_inputs, outputs, far_outputs=(), scratch=(), limit=24, flops=1 << 28):
    near, far = pl.BlockSpec(memory_space=pltpu.VMEM), pl.BlockSpec(memory_space=pl.ANY)
    return pl.pallas_call(
        body,
        out_shape=(*outputs, *far_outputs),
        in_specs=[near] * len(inputs) + [far] * len(far_inputs),
        out_specs=(near,) * len(outputs) + (far,) * len(far_outputs),
        scratch_shapes=list(scratch),
        compiler_params=pltpu.CompilerParams(vmem_limit_bytes=limit * 1024 * 1024),
        cost_estimate=pl.CostEstimate(flops=flops, bytes_accessed=1 << 20, transcendentals=0),
        name=name,
    )(*inputs, *far_inputs)


def array(dtype, *shape):
    return jax.ShapeDtypeStruct(shape, dtype)


def shifted(block, axis, distance):
    devices = range(lax.axis_size(axis))
    route = [(i - distance, i) for i in devices if i - distance in devices]
    return lax.ppermute(block, axis, route)


def diagonal(block):
    nd, nh = lax.axis_size("dev"), lax.axis_size("ha")
    route = [(i * nh + j, (i + 1) * nh + j + 1) for i in range(nd - 1) for j in range(nh - 1)]
    return lax.ppermute(block, ("dev", "ha"), route)


def mm(left, right):
    return jnp.dot(left, right, preferred_element_type=F32)


def mm_nt(left, right):
    return lax.dot_general(left, right, (((1,), (1,)), ((), ())), preferred_element_type=F32)


def leaky_and_slope(z):
    u = 4.0 * z
    t = jnp.exp(-jnp.abs(u))
    s = 1.0 + t
    act = 0.3 * z + 0.175 * (jnp.maximum(u, 0.0) + jnp.log(s))
    r = 1.0 / s
    slope = 0.3 + 0.7 * jnp.where(u >= 0.0, r, t * r)
    return act, slope


def row_height(r):
    return np.where(r < 64, r % 16, (r - 64) % 8 - 8)


def row_channel(r):
    return np.where(r < 64, r // 16, (r - 64) // 8)


def constants(width):
    s = width // 8
    sel = np.zeros((width, 3 * 4 * s), np.float32)
    for e in range(3):
        for k, t in enumerate((0, 2, 1, 3)):
            for c in range(s):
                w = 8 * c + 2 * t - 1 + e
                if w >= 0:
                    sel[w, e * 4 * s + k * s + c] = 1
    r = np.arange(96)
    hot = np.zeros((11, 48, 288), np.float32)
    for j in range(11):
        for a in range(3):
            for b in range(3):
                for k in range(96):
                    if row_height(k) == 2 * (j - 3) - 1 + b:
                        hot[j, (a * 4 + row_channel(k)) * 3 + b, a * 96 + k] = 1
    cols = np.arange(288)
    a, r = cols // 96, cols % 96
    am = a * 4 + row_channel(r)
    j = np.arange(256) // 32
    spread_o = (np.arange(256)[:, None] % 32 == np.arange(32)[None]).astype(np.float32)
    spread_am = (np.arange(16)[:, None] == am[None]).astype(np.float32)
    mask = np.stack([(row_height(r)[:, None] == (2 * j - 1 + b)[None]) for b in range(3)]).astype(np.float32)
    later = np.zeros((2 * s, 2 * s), np.float32)
    for c in range(s):
        later[c, s + c] = 1
        if c + 1 < s:
            later[s + c, c + 1] = 1
    pair = np.zeros((4 * s, 6 * s), np.float32)
    for k in range(2):
        for c in range(s):
            pair[k * 2 * s + c, 2 * s + k * s + c] = 1
            pair[k * 2 * s + s + c, 4 * s + k * s + c] = 1
            if c + 1 < s:
                pair[k * 2 * s + s + c, k * s + c + 1] = 1
    spread = np.zeros((2 * s, 12 * s), np.float32)
    for k in range(2):
        for c in range(s):
            base = k * 6 * s
            spread[k * s + c, base + c] = 1
            spread[k * s + c, base + 2 * s + s + c] = 1
            if c > 0:
                spread[k * s + c, base + 4 * s + s + c - 1] = 1
    return {
        "sel": sel, "hot": hot, "spread_o": spread_o, "spread_am": spread_am, "mask": mask,
        "later": later, "pair": pair, "spread": spread,
    }


def first_body(
    wt_ref, later_ref, w2_ref, pair_ref, *refs,
):
    sources, refs = refs[:6], refs[6:]
    park_b, park_f = refs[:2]
    held, refs = refs[2:8], refs[8:]
    hot_ref, sel_ref, volume_ref, dd_ref, dz_ref, hz_ref = held
    (x1_ref, a1_ref, t_ref, a2_ref, x1_out, a1_out, slope1_ref, slope2_ref, x3_ref, sems, came) = refs
    fetches = [pltpu.make_async_copy(sources[i], held[i], came.at[i]) for i in range(6)]
    for fetch in fetches:
        fetch.start()
    sends = []

    def send(source, park, name):
        copy = pltpu.make_async_copy(source, parked(park, name, source.shape[1]), sems.at[len(sends)])
        copy.start()
        sends.append(copy)

    low_dev = (lax.axis_index("dev") > 0).astype(F32)
    low_ha = (lax.axis_index("ha") > 0).astype(F32)
    wt = wt_ref[...]
    fetches[0].wait()
    for j in range(11):
        part = mm(wt, hot_ref[j])
        t_ref[j * 32:j * 32 + 32] = jnp.concatenate([part[0:32], part[32:64], part[64:96]], 1).astype(BF)
    fetches[1].wait()
    sel = sel_ref[...]
    for volume, edges, first, skip, given in ((volume_ref, hz_ref, 7, 0, (2, 5)), (dd_ref, dz_ref, -1, 1, (3, 4))):
        for i in given:
            fetches[i].wait()
        side = mm(edges[...].reshape(256, -1), sel).astype(BF)
        main = [mm(volume[m, skip:].reshape((8 - skip) * 16, -1), sel).astype(BF) for m in range(4)]
        for d in range(skip, 8):
            base = (first + d) * 96
            for e in range(3):
                lanes = slice(e * 256, e * 256 + 256)
                for m in range(4):
                    x1_ref[e, base + m * 16:base + m * 16 + 16] = main[m][(d - skip) * 16:(d - skip) * 16 + 16, lanes]
                x1_ref[e, base + 64:base + 96] = side[d * 32:d * 32 + 32, lanes]
    for e in range(3):
        x1_out[e * 864:e * 864 + 864] = x1_ref[e, 576:1440]
    send(x1_out, park_b, "x1")
    t = t_ref[...]
    later = later_ref[...]
    for ii in range(7):
        lo = ii * 192
        z = mm(t, jnp.concatenate([x1_ref[e, lo:lo + 288] for e in range(3)], 0))
        act, slope = leaky_and_slope(z)
        rows = lax.broadcasted_iota(jnp.int32, act.shape, 0)
        keep = jnp.where(rows < 96, low_ha, 1.0)
        if ii < 3:
            keep = keep * low_dev
        act = (act * keep).astype(BF)
        a1_ref[ii, :, 128:384] = act
        a1_ref[ii, :, 0:128] = mm(act[:, 128:256], later).astype(BF)
        if ii >= 2:
            a1_out[(ii - 2) * 352:(ii - 1) * 352] = a1_ref[ii]
        if ii >= 3:
            slope1_ref[(ii - 3) * 256:(ii - 2) * 256] = slope[96:352]
    send(a1_out, park_b, "a1")
    send(slope1_ref, park_f, "slope1")

    def patch(p, q):
        return jnp.concatenate(
            [
                a1_ref[2 * p + 2 + a, (2 * q + 2 + b) * 32:(2 * q + 3 + b) * 32, e * 128:e * 128 + 128]
                for a in range(3) for b in range(3) for e in range(3)
            ], 0)

    w2t = w2_ref[...].astype(F32).T.astype(BF)
    for p in range(-1, 2):
        for group in ((-1, 0), (1, 2), (3,)):
            x = jnp.concatenate([patch(p, q) for q in group], 1)
            act, slope = leaky_and_slope(mm(w2t, x))
            for k, q in enumerate(group):
                part = act[:, k * 128:k * 128 + 128]
                if p < 0:
                    part = part * low_dev
                if q < 0:
                    part = part * low_ha
                a2_ref[p + 1, (q + 1) * 64:(q + 2) * 64] = part.astype(BF)
                if p >= 0 and q >= 0:
                    slope2_ref[p * 256 + q * 64:p * 256 + q * 64 + 64] = slope[:, k * 128:k * 128 + 128]
    send(slope2_ref, park_f, "slope2")
    for a in range(3):
        both = jnp.concatenate([a2_ref[a, 0:192], a2_ref[a, 128:320]], 1)
        spread = mm(both, pair_ref[...]).astype(BF)
        for b in range(3):
            for e in range(3):
                at = ((a * 3 + b) * 3 + e) * 64
                x3_ref[at:at + 64] = spread[b * 64:b * 64 + 64, e * 128:e * 128 + 128]
    send(x3_ref, park_b, "x3")
    for copy in sends:
        copy.wait()


def third_body(both_ref, order_ref, park_b, park_f, out_ref, d3_ref, g3_ref, sz_ref, sd_ref, x3_ref, slope2_ref, sems):
    fetches = (
        pltpu.make_async_copy(parked(park_b, "x3", 128), x3_ref, sems.at[0]),
        pltpu.make_async_copy(parked(park_f, "slope2", 128), slope2_ref, sems.at[1]),
    )
    for fetch in fetches:
        fetch.start()
    for fetch in fetches:
        fetch.wait()
    x3 = x3_ref[...]
    act, slope = leaky_and_slope(mm(both_ref[:, 128:1856], x3))
    out_ref[...] = act.astype(BF)
    d3 = (both_ref[:, 0:128].astype(F32) * slope).astype(BF)
    d3_ref[...] = d3
    sz_ref[0:128] = d3
    sd_ref[0:128] = d3
    for p in range(2):
        sz_ref[128 + 64 * p:192 + 64 * p] = slope2_ref[256 * p:256 * p + 64].astype(BF)
    sd_ref[128:384] = slope2_ref[0:256].astype(BF)
    ordered = mm(order_ref[...], d3).astype(BF)
    wide = jnp.concatenate([x3, jnp.zeros((64, 128), BF)], 0)
    g3 = mm_nt(ordered, wide).astype(BF)
    for k in range(14):
        g3_ref[k] = g3[:, k * 128:k * 128 + 128]
    g3_ref[14:16] = jnp.zeros((2, 128, 128), BF)


def sum_body(g3_ref, msg_ref, out_ref):
    nd, nh = out_ref.shape[0], out_ref.shape[1]
    g3 = jnp.sum(g3_ref[...].astype(F32), 0)
    msg = jnp.sum(msg_ref[...].astype(F32), 0)
    rows = g3.shape[0] // nh
    for h in range(nh):
        block = jnp.concatenate([g3[h * rows:(h + 1) * rows], msg], 0).astype(BF)
        for d in range(nd):
            out_ref[d, h] = block


def unpack_body(scales, total_ref, g1_ref, g2_ref, g3_ref):
    n, both, _ = total_ref.shape
    lot = 512 // n
    rows = both - lot
    slices = n // 16
    for tap in range(27):
        for s in range(slices):
            part = total_ref[tap // 2 * slices + s, 0:rows, tap % 2 * 64:tap % 2 * 64 + 64]
            g3_ref[tap, s * rows:(s + 1) * rows] = part.astype(F32) * scales[2]
    for k in range(2):
        part = total_ref[0:g2_ref.shape[1], rows:, k * 64:k * 64 + 64]
        g2_ref[k] = part.astype(F32) * scales[1]
    for block in range(3):
        lots = [total_ref[(432 + block * 16) // lot + i, rows:].astype(F32) for i in range(16 // lot)]
        part = jnp.concatenate(lots, 0) * scales[0]
        for k in range(4 if block < 2 else 1):
            for a in range(3):
                g1_ref[a * 9 + block * 4 + k] = part[a * 4:a * 4 + 4, k * 32:k * 32 + 32]


def backward_body(
    spread_ref, d3_ref, rz_ref, rd_ref, w3g_ref, w2_ref, later_ref, so_ref, sam_ref, mask_ref,
    park_b, park_f,
    msg_ref, d2_ref, d1_ref, slope2_ref, a1_ref, slope1_ref, x1_ref, sems,
):
    fetches = {}
    for i, (park, name, target) in enumerate(
            ((park_f, "slope2", slope2_ref), (park_b, "a1", a1_ref), (park_f, "slope1", slope1_ref), (park_b, "x1", x1_ref))):
        fetches[name] = pltpu.make_async_copy(parked(park, name, target.shape[1]), target, sems.at[i])
        fetches[name].start()
    spread = spread_ref[...]

    def blocks(pair, last):
        both = mm(pair, spread).astype(BF)
        lone = mm(last, spread[:, 0:384]).astype(BF)
        cols = [both[:, 0:384], both[:, 384:768], lone]
        return jnp.concatenate(
            [jnp.concatenate([c[:, e * 128:e * 128 + 128] for e in range(3)], 0) for c in cols], 1)

    u0 = mm(w3g_ref[192:576], blocks(d3_ref[...], rz_ref[0:128]))
    u1 = mm(w3g_ref[0:384], blocks(rd_ref[0:128], rd_ref[384:512]))
    u = {(0, 1): u0[0:192], (0, 2): u0[192:384], (1, 0): u1[0:192], (1, 1): u1[192:384]}
    fetches["slope2"].wait()
    taps = {0: ((1, 0),), 1: ((2, 0), (0, 1)), 2: ((1, 1),), 3: ((2, 1), (0, 2)), 4: ((1, 2),)}
    for x in range(3):
        for y in range(5):
            back = None
            for a, i in taps[x]:
                for b, j in taps[y]:
                    term = u[(i, a)][b * 64:b * 64 + 64, j * 128:j * 128 + 128]
                    back = term if back is None else back + term
            if x < 2 and y < 4:
                slope = slope2_ref[x * 256 + y * 64:x * 256 + y * 64 + 64]
            elif x < 2:
                slope = rz_ref[128 + 64 * x:192 + 64 * x].astype(F32)
            elif y < 4:
                slope = rd_ref[128 + 64 * y:192 + 64 * y].astype(F32)
            else:
                slope = rd_ref[512:576].astype(F32)
            d2_ref[x, :, y * 128:y * 128 + 128] = (back * slope).astype(BF)

    def at(p, a, q, b):
        return (2 * p + a) * 352 + (2 * q + b) * 32

    def patch(p, q):
        return jnp.concatenate(
            [
                a1_ref[at(p, a, q + 1, b):at(p, a, q + 1, b) + 32, e * 128:e * 128 + 128]
                for a in range(3) for b in range(3) for e in range(3)
            ], 0)

    fetches["a1"].wait()
    g2 = None
    for p in range(2):
        for q in (0, 2):
            x = jnp.concatenate([patch(p, q), patch(p, q + 1)], 1)
            term = mm_nt(x, d2_ref[p, :, q * 128:q * 128 + 256])
            g2 = term if g2 is None else g2 + term
    msg_ref[0:432] = jnp.concatenate([g2[0:432], g2[432:864]], 1).astype(BF)

    taps = w2_ref[...].reshape(9, 3, 32, 64)
    w2e = taps[:, 1].reshape(288, 64)
    w2o = jnp.concatenate([taps[:, 2].reshape(288, 64), taps[:, 0].reshape(288, 64)], 1)
    later = later_ref[...]
    ue, uo = {}, {}
    for p, first, end in ((0, 1, 3), (1, 0, 3), (2, 0, 1)):
        d2 = d2_ref[p]
        moved = jnp.concatenate(
            [mm_nt(d2[:, q * 128:q * 128 + 128], later).astype(BF) for q in range(5)], 1)
        e_part = mm(w2e[first * 96:end * 96], d2)
        o_part = mm(w2o[first * 96:end * 96], jnp.concatenate([d2, moved], 0))
        for a in range(first, end):
            lo = (a - first) * 96
            ue[(p, a)] = e_part[lo:lo + 96]
            uo[(p, a)] = o_part[lo:lo + 96]
    fetches["slope1"].wait()
    for x in range(4):
        for y in range(8):
            if y % 2 == 0:
                y_taps = ((1, y // 2),)
            else:
                y_taps = ((2, y // 2), (0, y // 2 + 1))
            x_taps = ((1, x // 2),) if x % 2 == 0 else ((2, x // 2), (0, x // 2 + 1))
            for k, source in ((0, ue), (1, uo)):
                back = None
                for a, p in x_taps:
                    for b, q in y_taps:
                        term = source[(p, a)][b * 32:b * 32 + 32, q * 128:q * 128 + 128]
                        back = term if back is None else back + term
                slope = slope1_ref[x * 256 + y * 32:x * 256 + y * 32 + 32, k * 128:k * 128 + 128]
                d1_ref[y * 32:y * 32 + 32, x * 256 + k * 128:x * 256 + k * 128 + 128] = (back * slope).astype(BF)

    d1 = d1_ref[...]
    so = so_ref[...]
    sam = sam_ref[...]
    columns = []
    fetches["x1"].wait()
    x = jnp.concatenate(
        [jnp.concatenate([x1_ref[e * 864 + i * 192:e * 864 + i * 192 + 288] for e in range(3)], 0) for i in range(4)], 1)
    wide = mm_nt(x, d1)
    grads = [wide[e * 288:e * 288 + 288] for e in range(3)]
    for b in range(3):
        for e in range(3):
            kept = grads[e] * mask_ref[b].astype(F32)
            high = kept.astype(BF)
            low = (kept - high.astype(F32)).astype(BF)
            columns.append(mm(high, so) + mm(low, so))
    wide = jnp.concatenate(columns, 1)
    high = wide.astype(BF)
    low = (wide - high.astype(F32)).astype(BF)
    g1 = (mm(sam, high) + mm(sam, low)).astype(BF)
    msg_ref[432:512] = jnp.zeros((80, 128), BF)
    msg_ref[432:448] = g1[:, 0:128]
    msg_ref[448:464] = g1[:, 128:256]
    msg_ref[464:480, 0:32] = g1[:, 256:288]


def local(volume, w_first, w_second, w_third, cotangent):
    nd, nh = lax.axis_size("dev"), lax.axis_size("ha")
    depth_total = volume.shape[1] * nd
    height_total = volume.shape[2] * nh
    width = volume.shape[3]
    cells = depth_total * height_total * width
    scale_first, scale_second, scale_third = (1.0 / math.sqrt(cells // 8 ** k) for k in (1, 2, 3))
    const = {k: jnp.asarray(v, BF) for k, v in constants(width).items()}
    vmem = pltpu.VMEM

    edge = volume[:, :, 8:].transpose(1, 0, 2, 3).reshape(8, 32, width)
    dd = shifted(volume, "dev", 1)
    dz = diagonal(edge)
    hz = shifted(edge, "ha", 1)

    share = cotangent[:, 0].reshape(-1, nh, 2, 64).transpose(1, 0, 2, 3).reshape(nh, -1, 128)
    piece = w_third.reshape(1728, -1).T
    both = jnp.concatenate([share, jnp.broadcast_to(piece[None], (nh,) + piece.shape)], 2)
    both = lax.all_to_all(both, "ha", 0, 0, tiled=True).reshape(128, 1856)
    wt = w_first.transpose(2, 4, 0, 3, 1).reshape(96, 36)
    wt = jnp.pad(wt, ((0, 0), (0, 12)))
    w2 = w_second.reshape(864, 64)
    dma = pltpu.SemaphoreType.DMA
    borrowed = [const["hot"], const["sel"], volume, dd, dz, hz]
    park_b, park_f = call(
        "first", first_body,
        [wt, const["later"], w2, const["pair"]], borrowed, [],
        [array(BF, *PARK_SHAPES[0]), array(F32, *PARK_SHAPES[1])],
        [*(vmem(x.shape, BF) for x in borrowed),
         vmem((3, 1440, 256), BF), vmem((7, 352, 384), BF), vmem((352, 864), BF), vmem((3, 320, 128), BF),
         vmem((2592, 256), BF), vmem((1760, 384), BF), vmem((1024, 256), F32), vmem((512, 128), F32),
         vmem((1728, 128), BF), dma((5,)), dma((6,))],
        63, 1 << 33)

    n = nd * nh
    slices = n // 16
    order = np.arange(128).reshape(nh, slices, -1).transpose(1, 0, 2).reshape(-1)
    order = jnp.asarray(np.eye(128)[order], BF)
    out3, d3, g3, sz, sd = call(
        "third", third_body, [both, order], [park_b, park_f],
        [array(BF, 128, 128), array(BF, 128, 128), array(BF, 16, 128, 128), array(BF, 256, 128), array(BF, 384, 128)],
        (), [vmem((1728, 128), BF), vmem((512, 128), F32), dma((2,))], 8)

    g3_parts = lax.all_to_all(g3.reshape(n, 2048 // n, 128), ("dev", "ha"), 0, 0, tiled=True)
    rz = shifted(sz, "ha", -1)
    rd = shifted(jnp.concatenate([sd, rz[0:192]], 0), "dev", -1)

    share = lax.all_to_all(out3.reshape(nh, 128 // nh, 128), "ha", 0, 0, tiled=True)
    out_third = share.reshape(nh, 128 // nh, 2, 64).transpose(1, 0, 2, 3).reshape(128 // nh, 1, 2 * nh, 64)

    w3g = both[:, 128:].reshape(128, 9, 3, 64).transpose(1, 3, 2, 0)
    w3g = jnp.concatenate([w3g[:, :, 1], w3g[:, :, 2], w3g[:, :, 0]], 2).reshape(576, 384)
    msg, = call(
        "backward", backward_body,
        [const["spread"], d3, rz, rd, w3g, w2, const["later"], const["spread_o"], const["spread_am"], const["mask"]],
        [park_b, park_f], [array(BF, 512, 128)], (),
        [vmem((3, 64, 640), BF), vmem((256, 1024), BF), vmem((512, 128), F32), vmem((1760, 384), BF),
         vmem((1024, 256), F32), vmem((2592, 256), BF), dma((4,))],
        24, 1 << 36)

    g3_parts, msg = lax.optimization_barrier((g3_parts, msg))
    msg_parts = lax.all_to_all(msg.reshape(n, 512 // n, 128), ("dev", "ha"), 0, 0, tiled=True)
    rows = 2048 // n // nh
    slices, = call("sum", sum_body, [g3_parts, msg_parts], [], [array(BF, nd, nh, rows + 512 // n, 128)], limit=8)
    total = lax.all_to_all(slices.reshape(n, rows + 512 // n, 128), ("dev", "ha"), 0, 0, tiled=True)
    scales = (scale_first, scale_second, scale_third)
    g1, g2, g3 = call(
        "unpack", functools.partial(unpack_body, scales), [total], [],
        [array(F32, 27, 4, 32), array(F32, 2, 432 * n // 512, 512 // n, 64), array(F32, 27, 128 // nh, 64)], limit=8)
    grad_first = g1.reshape(3, 3, 3, 4, 32)
    grad_second = g2.reshape(3, 3, 3, 32, 64)
    grad_third = g3.transpose(0, 2, 1).reshape(3, 3, 3, 64, 128 // nh)
    return out_third, grad_first, grad_second, grad_third


def solution(mesh):
    placed = (
        P(None, "dev", "ha", None),
        P(),
        P(),
        P(None, None, None, None, "ha"),
        P("ha", "dev", None, None),
    )
    return jax.shard_map(
        local,
        mesh=mesh,
        in_specs=placed,
        out_specs=(P("ha", "dev", None, None), P(), P(), P(None, None, None, None, "ha")),
        check_vma=False,
    )
```

time: 137 us -> 100 us (0.73)
  blocking collectives: 49.3 us -> 12.3 us
  starting transfers between devices: 21.6 us -> 28.6 us
  local copies, waits for them, and re-layouts: 13.9 us -> 7.46 us
  Pallas kernels: 19.2 us -> 21.5 us
  waiting for transfers between devices: 29.3 us -> 27.9 us
    all_gather x2 -> x0, blocking collectives: 25.7 us -> none  [the longest x1 16.4 us: local(): w3t = lax.all_gather(w_third.reshape(1728, -1).T, 'ha', axis=0, tiled=True)]
    all_to_all x1 -> x0, blocking collectives: 10.1 us -> none  [local(): lax.all_to_all(spread, ('dev', 'ha'), 0, 0, tiled=True).reshape(512, 128)]
    unnamed x50 -> x19, local copies, waits for them, and re-layouts: 9.23 us -> 2.58 us
    ppermute x4, waiting for transfers between devices: 11.9 us -> 5.4 us  [shifted(): return lax.ppermute(block, axis, route)]
    all_to_all x2 -> x3, waiting for transfers between devices: 11.9 us -> 17.7 us  [the longest x1 9.43 us: local(): lax.all_to_all(slices.reshape(n, rows + 512 // n, 128), ('dev', 'ha'), 0,...]
    ppermute x0 -> x1, starting transfers between devices: none -> 4.91 us  [diagonal(): return lax.ppermute(block, ('dev', 'ha'), route)]
    all_to_all x2 -> x3, starting transfers between devices: 8.38 us -> 11.1 us  [the longest x1 5.08 us: local(): lax.all_to_all(g3.reshape(n, 2048 // n, 128), ('dev', 'ha'), 0, 0, tiled=...]
    pallas_call x3 -> x5, Pallas kernels: 19.2 us -> 21.5 us  [call(): pl.pallas_call(body, out_shape=(*outputs, *far_outputs), in_specs=[near]...]
  transfers between devices with their start and end apart: 7 -> 9, of which waited for: 5 -> 6; matrix products, arithmetic and copies ran while one was open for 5% -> 7% of each run, Pallas kernels for 2% -> 18%
where the time goes in v1:
time: 100 us; the launch traced here: 99.4 us
  starting transfers between devices  28.6 us (29%)
  waiting for transfers between devices  27.9 us (28%)
  Pallas kernels  21.5 us (22%)
  blocking collectives  12.3 us (12%)
  local copies, waits for them, and re-layouts  7.46 us (7%)
    pallas_call x5, Pallas kernels, call(): pl.pallas_call(body, out_shape=(*outputs, *far_outputs), in_specs=[near]...  21.5 us
    all_to_all x1, blocking collectives, local(): lax.all_to_all(msg.reshape(n, 512 // n, 128), ('dev', 'ha'), 0, 0, tiled=...  12.3 us
    all_to_all x1, waiting for transfers between devices, local(): lax.all_to_all(slices.reshape(n, rows + 512 // n, 128), ('dev', 'ha'), 0,...  9.43 us
    ppermute x4, starting transfers between devices, shifted(): return lax.ppermute(block, axis, route)  9.25 us
    all_to_all x1, waiting for transfers between devices, local(): lax.all_to_all(g3.reshape(n, 2048 // n, 128), ('dev', 'ha'), 0, 0, tiled=...  8.08 us
    ppermute x4, waiting for transfers between devices, shifted(): return lax.ppermute(block, axis, route)  5.4 us
    all_to_all x1, starting transfers between devices, local(): lax.all_to_all(g3.reshape(n, 2048 // n, 128), ('dev', 'ha'), 0, 0, tiled=...  5.08 us
    ppermute x1, starting transfers between devices, diagonal(): return lax.ppermute(block, ('dev', 'ha'), route)  4.91 us
  transfers between devices with their start and end apart: 9, of which 6 were waited for; matrix products, arithmetic and copies ran while one was open for 7% of the time, Pallas kernels for 18%

profile of v1, /device:TPU:0, one launch (start us, length us, event | category | flops | bytes accessed | tf_op | source)
XLA Modules:
  0.0 99.4 jit_solution(4483261153558446824)
XLA Ops:
  0.6 3.2 %collective-permute-start = (bf16[4,8,16,512]{3,2,1,0:T(8,128)(2,1)}, bf16[4,8,16,512]{3,2,1,0:T(8,128)(2,1)}, u32[]{:S(2)}, u32[]{:S(2)}) collective-permute-start(bf16[4,8,16,512]{3,2,1,0:T(8,128)(2,1)} %refs_2_.1), channel_id=1, source_target_pairs={{0,4},{4,8},{8,12},{12,16},{16,20},{20,24},{24,28},{1,5},{5,9},{9,... | collective-permute-start | bytes 1572872 | tf_op jit(solution)/shard_map/ppermute | solution.py:44
  3.8 1.0 copy_bitcast_fusion
  4.8 4.9 %collective-permute-start.1 = (bf16[8,32,512]{2,1,0:T(8,128)(2,1)S(1)}, bf16[8,32,512]{2,1,0:T(8,128)(2,1)S(1)}, u32[]{:S(2)}, u32[]{:S(2)}) collective-permute-start(bf16[8,32,512]{2,1,0:T(8,128)(2,1)S(1)} %copy_bitcast_fusion), channel_id=1, source_target_pairs={{0,5},{1,6},{2,7},{4,9},{5,10},{6,11},{8,13},{9,14},{10,15},{12,17... | collective-permute-start | bytes 786440 | tf_op jit(solution)/shard_map/ppermute | solution.py:50
  9.7 3.5 %collective-permute-start.2 = (bf16[8,32,512]{2,1,0:T(8,128)(2,1)S(1)}, bf16[8,32,512]{2,1,0:T(8,128)(2,1)S(1)}, u32[]{:S(2)}, u32[]{:S(2)}) collective-permute-start(bf16[8,32,512]{2,1,0:T(8,128)(2,1)S(1)} %copy_bitcast_fusion), channel_id=1, source_target_pairs={{0,1},{1,2},{2,3},{4,5},{5,6},{6,7},{8,9},{9,10},{10,11},{12,13},{... | collective-permute-start | bytes 786440 | tf_op jit(solution)/shard_map/ppermute | solution.py:44
  13.2 1.1 %copy.24 = bf16[3,3,3,64,32]{3,2,1,0,4:T(4,128)(2,1)S(1)} copy(bf16[3,3,3,64,32]{3,4,2,1,0:T(8,128)(2,1)} %param.17) | data formatting | bytes 221184 | tf_op args[3]
  14.3 0.2 reshape.65
  14.5 0.9 reshape.80
  15.5 0.8 pad_maximum_fusion
  16.3 3.5 %all-to-all-start = ((bf16[4,32,1856]{2,1,0:T(8,128)(2,1)}), bf16[4,32,1856]{2,1,0:T(8,128)(2,1)S(1)}, u32[]{:S(2)}, u32[]{:S(2)}) async-start(bf16[4,32,1856]{2,1,0:T(8,128)(2,1)} %pad_maximum_fusion), calls=%async_computation | async-start | bytes 983040 | tf_op jit(solution)/shard_map/all_to_all | solution.py:418
  19.8 0.8 copy.25
  20.8 0.6 pad.4.wt_ref
  21.4 0.5 collective-permute-done.2.refs_5_
  22.0 0.7 copy-done.8
  22.7 10.7 %first.1 = (bf16[90112,384]{1,0:T(8,128)(2,1)}, f32[67584,256]{1,0:T(8,128)}) custom-call(bf16[96,48]{1,0:T(8,128)(2,1)} %pad.4.wt_ref, bf16[128,128]{1,0:T(8,128)(2,1)} %constant.26.clone.later_ref, bf16[864,64]{1,0:T(8,128)(2,1)} %bitcast.39, bf16[256,384]{1,0:T(8,128)(2,1)} %constant.27.clone.pair_ref, bf16[11,48,288]{2,1,0:T(8,128)(2,1)} %constant.22.clone.refs_0_, ...), custom_call_target="tpu_custom_call" | custom-call | flops 8589934592 | bytes 1048576 | tf_op jit(solution)/shard_map/first/pallas_call | solution.py:25
  33.4 0.2 all-to-all-done
  33.5 0.8 copy-done
  34.3 2.7 %third.1 = (bf16[128,128]{1,0:T(8,128)(2,1)}, bf16[128,128]{1,0:T(8,128)(2,1)S(1)}, bf16[16,128,128]{2,1,0:T(8,128)(2,1)}, bf16[256,128]{1,0:T(8,128)(2,1)S(1)}, bf16[384,128]{1,0:T(8,128)(2,1)S(1)}) custom-call(bf16[128,1856]{1,0:T(8,128)(2,1)S(1)} %bitcast.36, bf16[128,128]{1,0:T(8,128)(2,1)S(1)} %copy-done, bf16[90112,384]{1,0:T(8,128)(2,1)} %get-tuple-element.16.park_b, ...), custom_call_target="tpu_custom_call" | custom-call | flops 268435456 | bytes 1048576 | tf_op jit(solution)/shard_map/third/pallas_call | solution.py:25
  37.1 1.3 %collective-permute-start.3 = (bf16[256,128]{1,0:T(8,128)(2,1)S(1)}, bf16[256,128]{1,0:T(8,128)(2,1)S(1)}, u32[]{:S(2)}, u32[]{:S(2)}) collective-permute-start(bf16[256,128]{1,0:T(8,128)(2,1)S(1)} %get-tuple-element.21), channel_id=1, source_target_pairs={{1,0},{2,1},{3,2},{5,4},{6,5},{7,6},{9,8},{10,9},{11,10},{13,12},{... | collective-permute-start | bytes 196616 | tf_op jit(solution)/shard_map/ppermute | solution.py:44
  38.4 0.3 copy.29
  38.7 4.9 %collective-permute-done.3.rz_ref = bf16[256,128]{1,0:T(8,128)(2,1)S(1)} collective-permute-done((bf16[256,128]{1,0:T(8,128)(2,1)S(1)}, bf16[256,128]{1,0:T(8,128)(2,1)S(1)}, u32[]{:S(2)}, u32[]{:S(2)}) %collective-permute-start.3) | collective-permute-done | bytes 65568 | tf_op jit(solution)/shard_map/ppermute | solution.py:44
  43.6 1.3 %collective-permute-start.4 = (bf16[576,128]{1,0:T(8,128)(2,1)S(1)}, bf16[576,128]{1,0:T(8,128)(2,1)S(1)}, u32[]{:S(2)}, u32[]{:S(2)}) collective-permute-start(bf16[576,128]{1,0:T(8,128)(2,1)S(1)} %pad_maximum_fusion.2), channel_id=1, source_target_pairs={{4,0},{8,4},{12,8},{16,12},{20,16},{24,20},{28,24},{5,1},{9,5},{13... | collective-permute-start | bytes 442376 | tf_op jit(solution)/shard_map/ppermute | solution.py:44
  44.9 5.1 %all-to-all-start.2 = ((bf16[32,64,128]{2,1,0:T(8,128)(2,1)}), bf16[32,64,128]{2,1,0:T(8,128)(2,1)S(1)}, u32[]{:S(2)}, u32[]{:S(2)}) async-start(bf16[32,64,128]{2,1,0:T(8,128)(2,1)} %bitcast.11), calls=%async_computation.2 | async-start | bytes 1048576 | tf_op jit(solution)/shard_map/all_to_all | solution.py:443
  50.1 6.1 %backward.1 = bf16[512,128]{1,0:T(8,128)(2,1)S(1)} custom-call(bf16[128,768]{1,0:T(8,128)(2,1)S(1)} %copy-done.3, bf16[128,128]{1,0:T(8,128)(2,1)S(1)} %get-tuple-element.20.d3_ref, bf16[256,128]{1,0:T(8,128)(2,1)S(1)} %collective-permute-done.3.rz_ref, bf16[576,128]{1,0:T(8,128)(2,1)S(1)} %collective-permute-done.4.rd_ref, ...), custom_call_target="tpu_custom_call" | custom-call | flops 68719476736 | bytes 1048576 | tf_op jit(solution)/shard_map/backward/pallas_call | solution.py:25
  56.3 8.1 %all-to-all-done.2.g3_ref = bf16[32,64,128]{2,1,0:T(8,128)(2,1)S(1)} async-done(((bf16[32,64,128]{2,1,0:T(8,128)(2,1)}), bf16[32,64,128]{2,1,0:T(8,128)(2,1)S(1)}, u32[]{:S(2)}, u32[]{:S(2)}) %all-to-all-start.2) | async-done | bytes 524320 | tf_op jit(solution)/shard_map/all_to_all | solution.py:443
  64.4 12.3 %all_to_all.25.msg_ref = bf16[32,16,128]{2,1,0:T(8,128)(2,1)S(1)} all-to-all(bf16[32,16,128]{2,1,0:T(8,128)(2,1)S(1)} %bitcast.38), channel_id=1, replica_groups=mesh['dev'=8,'ha'=4] {'dev','ha'}, dimensions={0} | all-to-all | bytes 262144 | tf_op jit(solution)/shard_map/all_to_all | solution.py:461
  76.6 3.3 %all-to-all-start.1 = ((bf16[4,32,128]{2,1,0:T(8,128)(2,1)}), bf16[4,32,128]{2,1,0:T(8,128)(2,1)S(1)}, u32[]{:S(2)}, u32[]{:S(2)}) async-start(bf16[4,32,128]{2,1,0:T(8,128)(2,1)} %bitcast.8), calls=%async_computation.1 | async-start | bytes 65536 | tf_op jit(solution)/shard_map/all_to_all | solution.py:447
  79.9 0.8 sum.1
  80.7 4.8 %all-to-all-done.1 = bf16[4,32,128]{2,1,0:T(8,128)(2,1)S(1)} async-done(((bf16[4,32,128]{2,1,0:T(8,128)(2,1)}), bf16[4,32,128]{2,1,0:T(8,128)(2,1)S(1)}, u32[]{:S(2)}, u32[]{:S(2)}) %all-to-all-start.1) | async-done | bytes 32800 | tf_op jit(solution)/shard_map/all_to_all | solution.py:447
  85.5 2.6 %all-to-all-start.4 = ((bf16[32,32,128]{2,1,0:T(8,128)(2,1)}), bf16[32,32,128]{2,1,0:T(8,128)(2,1)S(1)}, u32[]{:S(2)}, u32[]{:S(2)}) async-start(bf16[32,32,128]{2,1,0:T(8,128)(2,1)} %bitcast.19), calls=%async_computation.4 | async-start | bytes 524288 | tf_op jit(solution)/shard_map/all_to_all | solution.py:464
  88.2 0.7 copy.28
  88.9 9.4 %all-to-all-done.4.total_ref = bf16[32,32,128]{2,1,0:T(8,128)(2,1)S(1)} async-done(((bf16[32,32,128]{2,1,0:T(8,128)(2,1)}), bf16[32,32,128]{2,1,0:T(8,128)(2,1)S(1)}, u32[]{:S(2)}, u32[]{:S(2)}) %all-to-all-start.4) | async-done | bytes 262176 | tf_op jit(solution)/shard_map/all_to_all | solution.py:464
  98.3 1.1 %unpack.1 = (f32[27,4,32]{2,1,0:T(4,128)}, f32[2,27,16,64]{3,2,1,0:T(8,128)}, f32[27,32,64]{2,1,0:T(8,128)}) custom-call(bf16[32,32,128]{2,1,0:T(8,128)(2,1)S(1)} %all-to-all-done.4.total_ref), custom_call_target="tpu_custom_call" | custom-call | flops 268435456 | bytes 1048576 | tf_op jit(solution)/shard_map/unpack/pallas_call | solution.py:25
  (29 shorter events, 0.5 us)
Async XLA Ops:
  0.6 22.0 %collective-permute-start = (bf16[4,8,16,512]{3,2,1,0:T(8,128)(2,1)}, bf16[4,8,16,512]{3,2,1,0:T(8,128)(2,1)}, u32[]{:S(2)}, u32[]{:S(2)}) collective-permute-start(bf16[4,8,16,512]{3,2,1,0:T(8,128)(2,1)} %refs_2_.1), channel_id=1, source_target_pairs={{0,4},{4,8},{8,12},{12,16},{16,20},{20,24},{24,28},{1,5},{5,9},{9,... | collective-permute-start | bytes 1572872 | tf_op jit(solution)/shard_map/ppermute | solution.py:44
  4.8 16.6 %collective-permute-start.1 = (bf16[8,32,512]{2,1,0:T(8,128)(2,1)S(1)}, bf16[8,32,512]{2,1,0:T(8,128)(2,1)S(1)}, u32[]{:S(2)}, u32[]{:S(2)}) collective-permute-start(bf16[8,32,512]{2,1,0:T(8,128)(2,1)S(1)} %copy_bitcast_fusion), channel_id=1, source_target_pairs={{0,5},{1,6},{2,7},{4,9},{5,10},{6,11},{8,13},{9,14},{10,15},{12,17... | collective-permute-start | bytes 786440 | tf_op jit(solution)/shard_map/ppermute | solution.py:50
  9.7 12.3 %collective-permute-start.2 = (bf16[8,32,512]{2,1,0:T(8,128)(2,1)S(1)}, bf16[8,32,512]{2,1,0:T(8,128)(2,1)S(1)}, u32[]{:S(2)}, u32[]{:S(2)}) collective-permute-start(bf16[8,32,512]{2,1,0:T(8,128)(2,1)S(1)} %copy_bitcast_fusion), channel_id=1, source_target_pairs={{0,1},{1,2},{2,3},{4,5},{5,6},{6,7},{8,9},{9,10},{10,11},{12,13},{... | collective-permute-start | bytes 786440 | tf_op jit(solution)/shard_map/ppermute | solution.py:44
  16.3 17.2 %all-to-all-start = ((bf16[4,32,1856]{2,1,0:T(8,128)(2,1)}), bf16[4,32,1856]{2,1,0:T(8,128)(2,1)S(1)}, u32[]{:S(2)}, u32[]{:S(2)}) async-start(bf16[4,32,1856]{2,1,0:T(8,128)(2,1)} %pad_maximum_fusion), calls=%async_computation | async-start | bytes 983040 | tf_op jit(solution)/shard_map/all_to_all | solution.py:418
  21.4 1.3 %copy-start.7 = (bf16[8,32,512]{2,1,0:T(8,128)(2,1)}, bf16[8,32,512]{2,1,0:T(8,128)(2,1)S(1)}, u32[]{:S(2)}) copy-start(bf16[8,32,512]{2,1,0:T(8,128)(2,1)S(1)} %collective-permute-done.1.refs_4_) | copy-start | bytes 786436
  22.0 0.7 copy-start.8
  33.5 0.8 copy-start
  34.3 15.8 %copy-start.1 = (bf16[3,3,3,32,64]{4,3,2,1,0:T(8,128)(2,1)S(1)}, bf16[3,3,3,32,64]{4,3,2,1,0:T(8,128)(2,1)}, u32[]{:S(2)}) copy-start(bf16[3,3,3,32,64]{4,3,2,1,0:T(8,128)(2,1)} %param.16) | copy-start | bytes 331780
  34.3 15.8 %copy-start.2 = (bf16[3,288,256]{2,1,0:T(8,128)(2,1)S(1)}, bf16[3,288,256]{2,1,0:T(8,128)(2,1)}, u32[]{:S(2)}) copy-start(bf16[3,288,256]{2,1,0:T(8,128)(2,1)} %constant.25.clone.mask_ref) | copy-start | bytes 1327108
  34.3 15.8 %copy-start.3 = (bf16[128,768]{1,0:T(8,128)(2,1)S(1)}, bf16[128,768]{1,0:T(8,128)(2,1)}, u32[]{:S(2)}) copy-start(bf16[128,768]{1,0:T(8,128)(2,1)} %constant.28.clone.spread_ref) | copy-start | bytes 589828
  34.3 15.8 %copy-start.4 = (bf16[256,32]{1,0:T(8,128)(2,1)S(1)}, bf16[256,32]{1,0:T(8,128)(2,1)}, u32[]{:S(2)}) copy-start(bf16[256,32]{1,0:T(8,128)(2,1)} %constant.23.clone.so_ref) | copy-start | bytes 49156
  34.3 15.8 %copy-start.5 = (bf16[128,128]{1,0:T(8,128)(2,1)S(1)}, bf16[128,128]{1,0:T(8,128)(2,1)}, u32[]{:S(2)}) copy-start(bf16[128,128]{1,0:T(8,128)(2,1)} %constant.26.clone.later_ref) | copy-start | bytes 98308
  34.3 15.8 %copy-start.6 = (bf16[16,288]{1,0:T(8,128)(2,1)S(1)}, bf16[16,288]{1,0:T(8,128)(2,1)}, u32[]{:S(2)}) copy-start(bf16[16,288]{1,0:T(8,128)(2,1)} %constant.24.clone.sam_ref) | copy-start | bytes 27652
  37.1 6.5 %collective-permute-start.3 = (bf16[256,128]{1,0:T(8,128)(2,1)S(1)}, bf16[256,128]{1,0:T(8,128)(2,1)S(1)}, u32[]{:S(2)}, u32[]{:S(2)}) collective-permute-start(bf16[256,128]{1,0:T(8,128)(2,1)S(1)} %get-tuple-element.21), channel_id=1, source_target_pairs={{1,0},{2,1},{3,2},{5,4},{6,5},{7,6},{9,8},{10,9},{11,10},{13,12},{... | collective-permute-start | bytes 196616 | tf_op jit(solution)/shard_map/ppermute | solution.py:44
  43.6 6.5 %collective-permute-start.4 = (bf16[576,128]{1,0:T(8,128)(2,1)S(1)}, bf16[576,128]{1,0:T(8,128)(2,1)S(1)}, u32[]{:S(2)}, u32[]{:S(2)}) collective-permute-start(bf16[576,128]{1,0:T(8,128)(2,1)S(1)} %pad_maximum_fusion.2), channel_id=1, source_target_pairs={{4,0},{8,4},{12,8},{16,12},{20,16},{24,20},{28,24},{5,1},{9,5},{13... | collective-permute-start | bytes 442376 | tf_op jit(solution)/shard_map/ppermute | solution.py:44
  44.9 19.5 %all-to-all-start.2 = ((bf16[32,64,128]{2,1,0:T(8,128)(2,1)}), bf16[32,64,128]{2,1,0:T(8,128)(2,1)S(1)}, u32[]{:S(2)}, u32[]{:S(2)}) async-start(bf16[32,64,128]{2,1,0:T(8,128)(2,1)} %bitcast.11), calls=%async_computation.2 | async-start | bytes 1048576 | tf_op jit(solution)/shard_map/all_to_all | solution.py:443
  76.6 8.9 %all-to-all-start.1 = ((bf16[4,32,128]{2,1,0:T(8,128)(2,1)}), bf16[4,32,128]{2,1,0:T(8,128)(2,1)S(1)}, u32[]{:S(2)}, u32[]{:S(2)}) async-start(bf16[4,32,128]{2,1,0:T(8,128)(2,1)} %bitcast.8), calls=%async_computation.1 | async-start | bytes 65536 | tf_op jit(solution)/shard_map/all_to_all | solution.py:447
  85.5 12.8 %all-to-all-start.4 = ((bf16[32,32,128]{2,1,0:T(8,128)(2,1)}), bf16[32,32,128]{2,1,0:T(8,128)(2,1)S(1)}, u32[]{:S(2)}, u32[]{:S(2)}) async-start(bf16[32,32,128]{2,1,0:T(8,128)(2,1)} %bitcast.19), calls=%async_computation.4 | async-start | bytes 524288 | tf_op jit(solution)/shard_map/all_to_all | solution.py:464

commit v2 on v1

--- a/solution.py
+++ b/solution.py
@@ -78,21 +78,6 @@
 
 def constants(width):
     s = width // 8
-    sel = np.zeros((width, 3 * 4 * s), np.float32)
-    for e in range(3):
-        for k, t in enumerate((0, 2, 1, 3)):
-            for c in range(s):
-                w = 8 * c + 2 * t - 1 + e
-                if w >= 0:
-                    sel[w, e * 4 * s + k * s + c] = 1
-    r = np.arange(96)
-    hot = np.zeros((11, 48, 288), np.float32)
-    for j in range(11):
-        for a in range(3):
-            for b in range(3):
-                for k in range(96):
-                    if row_height(k) == 2 * (j - 3) - 1 + b:
-                        hot[j, (a * 4 + row_channel(k)) * 3 + b, a * 96 + k] = 1
     cols = np.arange(288)
     a, r = cols // 96, cols % 96
     am = a * 4 + row_channel(r)
@@ -121,39 +106,73 @@
             if c > 0:
                 spread[k * s + c, base + 4 * s + s + c - 1] = 1
     return {
-        "sel": sel, "hot": hot, "spread_o": spread_o, "spread_am": spread_am, "mask": mask,
+        "spread_o": spread_o, "spread_am": spread_am, "mask": mask,
         "later": later, "pair": pair, "spread": spread,
     }
 
 
-def first_body(
-    wt_ref, later_ref, w2_ref, pair_ref, *refs,
-):
-    sources, refs = refs[:6], refs[6:]
+def deinterleave(width):
+    s = width // 8
+    col = lax.broadcasted_iota(jnp.int32, (1, 12 * s), 1)
+    k = col % (4 * s) // s
+    source = 8 * (col % s) + 2 * (k % 2 * 2 + k // 2) - 1 + col // (4 * s)
+    row = lax.broadcasted_iota(jnp.int32, (width, 12 * s), 0)
+    return jnp.where(row == source, 1.0, 0.0).astype(BF)
+
+
+def plane_taps(j):
+    col = lax.broadcasted_iota(jnp.int32, (1, 288), 1)
+    a = col // 96
+    r = col % 96
+    channel = jnp.where(r < 64, r // 16, (r - 64) // 8)
+    height = jnp.where(r < 64, r % 16, r % 8 - 8)
+    row = lax.broadcasted_iota(jnp.int32, (36, 1), 0)
+    want = (row // 12 * 4 + row % 4) * 64 + (2 * j - 1 + row // 4 % 3 + 32)
+    return jnp.where(want == (a * 4 + channel) * 64 + (height + 32), 1.0, 0.0).astype(BF)
+
+
+def prep_body(cot_ref, w3_ref, out_ref):
+    nh = out_ref.shape[0]
+    cot = cot_ref[...].astype(F32)
+    for k in range(14):
+        pair = [w3_ref[tap] for tap in (2 * k, 2 * k + 1) if tap < 27]
+        pair = jnp.concatenate(pair, 1) if len(pair) > 1 else pair[0]
+        for h in range(nh):
+            out_ref[h, :, 128 + k * 128:128 + k * 128 + pair.shape[1]] = pair
+    for h in range(nh):
+        out_ref[h, :, 0:128] = jnp.concatenate([cot[:, 2 * h], cot[:, 2 * h + 1]], 1).astype(BF)
+
+
+def first_body(*refs):
+    sources, refs = refs[:8], refs[8:]
     park_b, park_f = refs[:2]
-    held, refs = refs[2:8], refs[8:]
-    hot_ref, sel_ref, volume_ref, dd_ref, dz_ref, hz_ref = held
-    (x1_ref, a1_ref, t_ref, a2_ref, x1_out, a1_out, slope1_ref, slope2_ref, x3_ref, sems, came) = refs
-    fetches = [pltpu.make_async_copy(sources[i], held[i], came.at[i]) for i in range(6)]
+    held, refs = refs[2:10], refs[10:]
+    w1_ref, volume_ref, hz_ref, dd_ref, dz_ref, later_ref, w2_ref, pair_ref = held
+    (x1_ref, a1_ref, t_ref, a2_ref, slope1_ref, slope2_ref, x3_ref, sems, came) = refs
+    fetches = [pltpu.make_async_copy(sources[i], held[i], came.at[i]) for i in range(8)]
     for fetch in fetches:
         fetch.start()
     sends = []
 
-    def send(source, park, name):
-        copy = pltpu.make_async_copy(source, parked(park, name, source.shape[1]), sems.at[len(sends)])
+    def send(source, park, name, first=0):
+        rows, lanes = source.shape
+        first += PARK[name][0]
+        copy = pltpu.make_async_copy(source, park.at[first:first + rows, 0:lanes], sems.at[len(sends)])
         copy.start()
         sends.append(copy)
 
     low_dev = (lax.axis_index("dev") > 0).astype(F32)
     low_ha = (lax.axis_index("ha") > 0).astype(F32)
-    wt = wt_ref[...]
+    sel = deinterleave(volume_ref.shape[3])
+    taps = [plane_taps(j - 3) for j in range(11)]
     fetches[0].wait()
+    w1 = w1_ref[...].astype(F32)
+    w1 = jnp.concatenate([jnp.concatenate([w1[k * 3 + e] for k in range(9)], 0) for e in range(3)], 1)
+    wt = w1.T.astype(BF)
     for j in range(11):
-        part = mm(wt, hot_ref[j])
+        part = mm(wt, taps[j])
         t_ref[j * 32:j * 32 + 32] = jnp.concatenate([part[0:32], part[32:64], part[64:96]], 1).astype(BF)
-    fetches[1].wait()
-    sel = sel_ref[...]
-    for volume, edges, first, skip, given in ((volume_ref, hz_ref, 7, 0, (2, 5)), (dd_ref, dz_ref, -1, 1, (3, 4))):
+    for volume, edges, first, skip, given in ((volume_ref, hz_ref, 7, 0, (1, 2)), (dd_ref, dz_ref, -1, 1, (3, 4))):
         for i in given:
             fetches[i].wait()
         side = mm(edges[...].reshape(256, -1), sel).astype(BF)
@@ -166,9 +185,9 @@
                     x1_ref[e, base + m * 16:base + m * 16 + 16] = main[m][(d - skip) * 16:(d - skip) * 16 + 16, lanes]
                 x1_ref[e, base + 64:base + 96] = side[d * 32:d * 32 + 32, lanes]
     for e in range(3):
-        x1_out[e * 864:e * 864 + 864] = x1_ref[e, 576:1440]
-    send(x1_out, park_b, "x1")
+        send(x1_ref.at[e, 576:1440], park_b, "x1", e * 864)
     t = t_ref[...]
+    fetches[5].wait()
     later = later_ref[...]
     for ii in range(7):
         lo = ii * 192
@@ -179,22 +198,25 @@
         if ii < 3:
             keep = keep * low_dev
         act = (act * keep).astype(BF)
-        a1_ref[ii, :, 128:384] = act
-        a1_ref[ii, :, 0:128] = mm(act[:, 128:256], later).astype(BF)
-        if ii >= 2:
-            a1_out[(ii - 2) * 352:(ii - 1) * 352] = a1_ref[ii]
+        here = slice(ii * 352, ii * 352 + 352)
+        a1_ref[here, 128:384] = act
+        a1_ref[here, 0:128] = mm(act[:, 128:256], later).astype(BF)
         if ii >= 3:
             slope1_ref[(ii - 3) * 256:(ii - 2) * 256] = slope[96:352]
-    send(a1_out, park_b, "a1")
+    send(a1_ref.at[704:2464], park_b, "a1")
     send(slope1_ref, park_f, "slope1")
+
+    def at(p, a, q, b):
+        return (2 * p + a) * 352 + (2 * q + b) * 32
 
     def patch(p, q):
         return jnp.concatenate(
             [
-                a1_ref[2 * p + 2 + a, (2 * q + 2 + b) * 32:(2 * q + 3 + b) * 32, e * 128:e * 128 + 128]
+                a1_ref[at(p + 1, a, q + 1, b):at(p + 1, a, q + 1, b) + 32, e * 128:e * 128 + 128]
                 for a in range(3) for b in range(3) for e in range(3)
             ], 0)
 
+    fetches[6].wait()
     w2t = w2_ref[...].astype(F32).T.astype(BF)
     for p in range(-1, 2):
         for group in ((-1, 0), (1, 2), (3,)):
@@ -210,6 +232,7 @@
                 if p >= 0 and q >= 0:
                     slope2_ref[p * 256 + q * 64:p * 256 + q * 64 + 64] = slope[:, k * 128:k * 128 + 128]
     send(slope2_ref, park_f, "slope2")
+    fetches[7].wait()
     for a in range(3):
         both = jnp.concatenate([a2_ref[a, 0:192], a2_ref[a, 128:320]], 1)
         spread = mm(both, pair_ref[...]).astype(BF)
@@ -222,7 +245,8 @@
         copy.wait()
 
 
-def third_body(both_ref, order_ref, park_b, park_f, out_ref, d3_ref, g3_ref, sz_ref, sd_ref, x3_ref, slope2_ref, sems):
+def third_body(g3_slices, both_ref, park_b, park_f, d3_ref, kept_ref, given_ref, sz_ref, sd_ref, *refs):
+    blocks, (x3_ref, slope2_ref, out_ref, g3_ref, sems) = refs[:-5], refs[-5:]
     fetches = (
         pltpu.make_async_copy(parked(park_b, "x3", 128), x3_ref, sems.at[0]),
         pltpu.make_async_copy(parked(park_f, "slope2", 128), slope2_ref, sems.at[1]),
@@ -233,7 +257,11 @@
         fetch.wait()
     x3 = x3_ref[...]
     act, slope = leaky_and_slope(mm(both_ref[:, 128:1856], x3))
-    out_ref[...] = act.astype(BF)
+    out_ref[...] = act
+    nh, (ch, _) = len(blocks), blocks[0].shape
+    for k in range(nh):
+        owner = (lax.axis_index("ha") + k) % nh
+        blocks[k][...] = out_ref[pl.ds(pl.multiple_of(owner * ch, ch), ch)].astype(BF)
     d3 = (both_ref[:, 0:128].astype(F32) * slope).astype(BF)
     d3_ref[...] = d3
     sz_ref[0:128] = d3
@@ -241,21 +269,35 @@
     for p in range(2):
         sz_ref[128 + 64 * p:192 + 64 * p] = slope2_ref[256 * p:256 * p + 64].astype(BF)
     sd_ref[128:384] = slope2_ref[0:256].astype(BF)
-    ordered = mm(order_ref[...], d3).astype(BF)
+    slices = 128 // g3_slices
+    row = lax.broadcasted_iota(jnp.int32, (128, 1), 0)
+    source = row // slices % nh * ch + row // (nh * slices) * slices + row % slices
+    order = jnp.where(lax.broadcasted_iota(jnp.int32, (128, 128), 1) == source, 1.0, 0.0).astype(BF)
+    ordered = mm(order, d3).astype(BF)
     wide = jnp.concatenate([x3, jnp.zeros((64, 128), BF)], 0)
     g3 = mm_nt(ordered, wide).astype(BF)
     for k in range(14):
         g3_ref[k] = g3[:, k * 128:k * 128 + 128]
     g3_ref[14:16] = jnp.zeros((2, 128, 128), BF)
+    core = lax.axis_index("dev") % 2
+    kept_ref[...] = g3_ref[pl.ds(core * 8, 8)]
+    given_ref[...] = g3_ref[pl.ds(8 - core * 8, 8)]
+
+
+def collect_body(*refs):
+    blocks, out_ref = refs[:-1], refs[-1]
+    nh = len(blocks)
+    for k in range(nh):
+        out_ref[(lax.axis_index("ha") + nh - k) % nh] = blocks[k][...]
 
 
 def sum_body(g3_ref, msg_ref, out_ref):
     nd, nh = out_ref.shape[0], out_ref.shape[1]
-    g3 = jnp.sum(g3_ref[...].astype(F32), 0)
+    g3 = [sum(g3_ref[d * nh + h].astype(F32) for d in range(core, nd, 2) for h in range(nh)) for core in range(2)]
     msg = jnp.sum(msg_ref[...].astype(F32), 0)
-    rows = g3.shape[0] // nh
+    rows = g3[0].shape[0] // nh
     for h in range(nh):
-        block = jnp.concatenate([g3[h * rows:(h + 1) * rows], msg], 0).astype(BF)
+        block = jnp.concatenate([half[h * rows:(h + 1) * rows] for half in g3] + [msg], 0).astype(BF)
         for d in range(nd):
             out_ref[d, h] = block
 
@@ -263,17 +305,18 @@
 def unpack_body(scales, total_ref, g1_ref, g2_ref, g3_ref):
     n, both, _ = total_ref.shape
     lot = 512 // n
-    rows = both - lot
-    slices = n // 16
+    rows = (both - lot) // 2
+    slices = n // 8
     for tap in range(27):
         for s in range(slices):
-            part = total_ref[tap // 2 * slices + s, 0:rows, tap % 2 * 64:tap % 2 * 64 + 64]
+            lo = tap // 16 * rows
+            part = total_ref[tap % 16 // 2 * slices + s, lo:lo + rows, tap % 2 * 64:tap % 2 * 64 + 64]
             g3_ref[tap, s * rows:(s + 1) * rows] = part.astype(F32) * scales[2]
     for k in range(2):
-        part = total_ref[0:g2_ref.shape[1], rows:, k * 64:k * 64 + 64]
+        part = total_ref[0:g2_ref.shape[1], 2 * rows:, k * 64:k * 64 + 64]
         g2_ref[k] = part.astype(F32) * scales[1]
     for block in range(3):
-        lots = [total_ref[(432 + block * 16) // lot + i, rows:].astype(F32) for i in range(16 // lot)]
+        lots = [total_ref[(432 + block * 16) // lot + i, 2 * rows:].astype(F32) for i in range(16 // lot)]
         part = jnp.concatenate(lots, 0) * scales[0]
         for k in range(4 if block < 2 else 1):
             for a in range(3):
@@ -412,40 +455,38 @@
     dz = diagonal(edge)
     hz = shifted(edge, "ha", 1)
 
-    share = cotangent[:, 0].reshape(-1, nh, 2, 64).transpose(1, 0, 2, 3).reshape(nh, -1, 128)
-    piece = w_third.reshape(1728, -1).T
-    both = jnp.concatenate([share, jnp.broadcast_to(piece[None], (nh,) + piece.shape)], 2)
+    ch = 128 // nh
+    natural = w_third.transpose(0, 1, 2, 4, 3).reshape(27, ch, 64)
+    both, = call("prep", prep_body, [cotangent[:, 0], natural], [], [array(BF, nh, ch, 1856)], limit=8)
     both = lax.all_to_all(both, "ha", 0, 0, tiled=True).reshape(128, 1856)
-    wt = w_first.transpose(2, 4, 0, 3, 1).reshape(96, 36)
-    wt = jnp.pad(wt, ((0, 0), (0, 12)))
     w2 = w_second.reshape(864, 64)
     dma = pltpu.SemaphoreType.DMA
-    borrowed = [const["hot"], const["sel"], volume, dd, dz, hz]
+    loaded = [w_first.reshape(27, 4, 32), volume, hz, dd, dz, const["later"], w2, const["pair"]]
     park_b, park_f = call(
         "first", first_body,
-        [wt, const["later"], w2, const["pair"]], borrowed, [],
+        [], loaded, [],
         [array(BF, *PARK_SHAPES[0]), array(F32, *PARK_SHAPES[1])],
-        [*(vmem(x.shape, BF) for x in borrowed),
-         vmem((3, 1440, 256), BF), vmem((7, 352, 384), BF), vmem((352, 864), BF), vmem((3, 320, 128), BF),
-         vmem((2592, 256), BF), vmem((1760, 384), BF), vmem((1024, 256), F32), vmem((512, 128), F32),
-         vmem((1728, 128), BF), dma((5,)), dma((6,))],
+        [*(vmem(x.shape, BF) for x in loaded),
+         vmem((3, 1440, 256), BF), vmem((2464, 384), BF), vmem((352, 864), BF), vmem((3, 320, 128), BF),
+         vmem((1024, 256), F32), vmem((512, 128), F32), vmem((1728, 128), BF), dma((7,)), dma((8,))],
         63, 1 << 33)
 
     n = nd * nh
-    slices = n // 16
-    order = np.arange(128).reshape(nh, slices, -1).transpose(1, 0, 2).reshape(-1)
-    order = jnp.asarray(np.eye(128)[order], BF)
-    out3, d3, g3, sz, sd = call(
-        "third", third_body, [both, order], [park_b, park_f],
-        [array(BF, 128, 128), array(BF, 128, 128), array(BF, 16, 128, 128), array(BF, 256, 128), array(BF, 384, 128)],
-        (), [vmem((1728, 128), BF), vmem((512, 128), F32), dma((2,))], 8)
-
-    g3_parts = lax.all_to_all(g3.reshape(n, 2048 // n, 128), ("dev", "ha"), 0, 0, tiled=True)
+    d3, kept, given, sz, sd, *blocks = call(
+        "third", functools.partial(third_body, nh * (n // 8)), [both], [park_b, park_f],
+        [array(BF, 128, 128), array(BF, 8, 128, 128), array(BF, 8, 128, 128), array(BF, 256, 128), array(BF, 384, 128), *[array(BF, ch, 128)] * nh],
+        (), [vmem((1728, 128), BF), vmem((512, 128), F32), vmem((128, 128), F32), vmem((16, 128, 128), BF), dma((2,))], 8)
+
+    given = lax.ppermute(given, "dev", [(i, i ^ 1) for i in range(nd)])
+    halves = (kept.astype(F32) + given.astype(F32)).astype(BF)
+    g3_parts = lax.all_to_all(halves.reshape(n, 1024 // n, 128), ("dev", "ha"), 0, 0, tiled=True)
     rz = shifted(sz, "ha", -1)
     rd = shifted(jnp.concatenate([sd, rz[0:192]], 0), "dev", -1)
 
-    share = lax.all_to_all(out3.reshape(nh, 128 // nh, 128), "ha", 0, 0, tiled=True)
-    out_third = share.reshape(nh, 128 // nh, 2, 64).transpose(1, 0, 2, 3).reshape(128 // nh, 1, 2 * nh, 64)
+    for k in range(1, nh):
+        blocks[k] = lax.ppermute(blocks[k], "ha", [(i, (i + k) % nh) for i in range(nh)])
+    share, = call("collect", collect_body, blocks, [], [array(BF, nh, ch, 128)], limit=4)
+    out_third = share.reshape(nh, ch, 2, 64).transpose(1, 0, 2, 3).reshape(ch, 1, 2 * nh, 64)
 
     w3g = both[:, 128:].reshape(128, 9, 3, 64).transpose(1, 3, 2, 0)
     w3g = jnp.concatenate([w3g[:, :, 1], w3g[:, :, 2], w3g[:, :, 0]], 2).reshape(576, 384)

time: 100 us -> 85.6 us (0.86)
  waiting for transfers between devices: 27.9 us -> 17.2 us
  local copies, waits for them, and re-layouts: 7.46 us -> 4.58 us
  starting transfers between devices: 28.6 us -> 30.2 us
  blocking collectives: 12.3 us -> 10.9 us
  Pallas kernels: 21.5 us -> 20.4 us
    all_to_all x1, waiting for transfers between devices: 9.43 us -> 0.01 us  [local(): lax.all_to_all(slices.reshape(n, rows + 512 // n, 128), ('dev', 'ha'), 0,...]
    all_to_all x2 -> x1, waiting for transfers between devices: 12.9 us -> 3.97 us  [local(): lax.all_to_all(halves.reshape(n, 1024 // n, 128), ('dev', 'ha'), 0, 0, ti...]
    ppermute x0 -> x4, starting transfers between devices: none -> 5.7 us  [the longest x3 5.63 us: local(): lax.ppermute(blocks[k], 'ha', [(i, (i + k) % nh) for i in range(nh)])]
    ppermute x0 -> x4, waiting for transfers between devices: none -> 4.35 us  [the longest x3 4.35 us: local(): lax.ppermute(blocks[k], 'ha', [(i, (i + k) % nh) for i in range(nh)])]
    all_to_all x2 -> x1, starting transfers between devices: 8.35 us -> 4.6 us  [local(): lax.all_to_all(halves.reshape(n, 1024 // n, 128), ('dev', 'ha'), 0, 0, ti...]
    ppermute x1, waiting for transfers between devices: 0.01 us -> 2.26 us  [diagonal(): return lax.ppermute(block, ('dev', 'ha'), route)]
    reshape x7 -> x1, local copies, waits for them, and re-layouts: 2.14 us -> 0.09 us  [local(): share.reshape(nh, ch, 2, 64).transpose(1, 0, 2, 3)]
    all_to_all x1, waiting for transfers between devices: 0.17 us -> 1.89 us  [local(): both = lax.all_to_all(both, 'ha', 0, 0, tiled=True).reshape(128, 1856)]
  transfers between devices with their start and end apart: 9 -> 12, of which waited for: 6 -> 6; matrix products, arithmetic and copies ran while one was open for 7% -> 3% of each run, Pallas kernels for 18% -> 19%
where the time goes in v2:
time: 85.6 us; the launch traced here: 85 us
  starting transfers between devices  30.2 us (35%)
  Pallas kernels  20.4 us (24%)
  waiting for transfers between devices  17.2 us (20%)
  blocking collectives  10.9 us (13%)
  local copies, waits for them, and re-layouts  4.58 us (5%)
  between operations  0.9 us (1%)
    pallas_call x7, Pallas kernels, call(): pl.pallas_call(body, out_shape=(*outputs, *far_outputs), in_specs=[near]...  20.4 us
    all_to_all x1, blocking collectives, local(): lax.all_to_all(msg.reshape(n, 512 // n, 128), ('dev', 'ha'), 0, 0, tiled=...  10.9 us
    ppermute x4, starting transfers between devices, shifted(): return lax.ppermute(block, axis, route)  10.1 us
    ppermute x3, starting transfers between devices, local(): lax.ppermute(blocks[k], 'ha', [(i, (i + k) % nh) for i in range(nh)])  5.63 us
    ppermute x4, waiting for transfers between devices, shifted(): return lax.ppermute(block, axis, route)  4.71 us
    all_to_all x1, starting transfers between devices, local(): lax.all_to_all(halves.reshape(n, 1024 // n, 128), ('dev', 'ha'), 0, 0, ti...  4.6 us
    ppermute x3, waiting for transfers between devices, local(): lax.ppermute(blocks[k], 'ha', [(i, (i + k) % nh) for i in range(nh)])  4.35 us
    all_to_all x1, waiting for transfers between devices, local(): lax.all_to_all(halves.reshape(n, 1024 // n, 128), ('dev', 'ha'), 0, 0, ti...  3.97 us
  transfers between devices with their start and end apart: 12, of which 6 were waited for; matrix products, arithmetic and copies ran while one was open for 3% of the time, Pallas kernels for 19%

profile of v2, /device:TPU:0, one launch (start us, length us, event | category | flops | bytes accessed | tf_op | source)
XLA Modules:
  0.0 85.0 jit_solution(5969708742411951257)
XLA Ops:
  0.6 3.2 %collective-permute-start.1 = (bf16[4,8,16,512]{3,2,1,0:T(8,128)(2,1)}, bf16[4,8,16,512]{3,2,1,0:T(8,128)(2,1)}, u32[]{:S(2)}, u32[]{:S(2)}) collective-permute-start(bf16[4,8,16,512]{3,2,1,0:T(8,128)(2,1)} %refs_1_.1), channel_id=1, source_target_pairs={{0,4},{4,8},{8,12},{12,16},{16,20},{20,24},{24,28},{1,5},{5,9},{9,... | collective-permute-start | bytes 1572872 | tf_op jit(solution)/shard_map/ppermute | solution.py:44
  3.8 1.0 %copy_bitcast_fusion = bf16[8,32,512]{2,1,0:T(8,128)(2,1)S(1)} fusion(bf16[4,8,16,512]{3,2,1,0:T(8,128)(2,1)} %refs_1_.1), kind=kLoop, calls=%fused_computation.2 | loop fusion | bytes 524288 | tf_op jit(solution)/shard_map/reshape | solution.py:453
  4.8 4.3 %collective-permute-start = (bf16[8,32,512]{2,1,0:T(8,128)(2,1)S(1)}, bf16[8,32,512]{2,1,0:T(8,128)(2,1)S(1)}, u32[]{:S(2)}, u32[]{:S(2)}) collective-permute-start(bf16[8,32,512]{2,1,0:T(8,128)(2,1)S(1)} %copy_bitcast_fusion), channel_id=1, source_target_pairs={{0,1},{1,2},{2,3},{4,5},{5,6},{6,7},{8,9},{9,10},{10,11},{12,13},{... | collective-permute-start | bytes 786440 | tf_op jit(solution)/shard_map/ppermute | solution.py:44
  9.1 3.8 %collective-permute-start.2 = (bf16[8,32,512]{2,1,0:T(8,128)(2,1)S(1)}, bf16[8,32,512]{2,1,0:T(8,128)(2,1)S(1)}, u32[]{:S(2)}, u32[]{:S(2)}) collective-permute-start(bf16[8,32,512]{2,1,0:T(8,128)(2,1)S(1)} %copy_bitcast_fusion), channel_id=1, source_target_pairs={{0,5},{1,6},{2,7},{4,9},{5,10},{6,11},{8,13},{9,14},{10,15},{12,17... | collective-permute-start | bytes 786440 | tf_op jit(solution)/shard_map/ppermute | solution.py:50
  12.9 0.9 %copy-done = bf16[3,3,3,64,32]{3,4,2,1,0:T(8,128)(2,1)S(1)} copy-done((bf16[3,3,3,64,32]{3,4,2,1,0:T(8,128)(2,1)S(1)}, bf16[3,3,3,64,32]{3,4,2,1,0:T(8,128)(2,1)}, u32[]{:S(2)}) %copy-start) | copy-done | bytes 110616
  13.8 0.8 copy-done.2
  14.7 0.9 %prep.1 = bf16[4,32,1856]{2,1,0:T(8,128)(2,1)} custom-call(bf16[32,8,64]{2,1,0:T(8,128)(2,1)S(1)} %bitcast.34, bf16[27,32,64]{2,1,0:T(8,128)(2,1)S(1)} %bitcast.31), custom_call_target="tpu_custom_call" | custom-call | flops 268435456 | bytes 1048576 | tf_op jit(solution)/shard_map/prep/pallas_call | solution.py:25
  15.6 3.5 %all-to-all-start = ((bf16[4,32,1856]{2,1,0:T(8,128)(2,1)}), bf16[4,32,1856]{2,1,0:T(8,128)(2,1)S(1)}, u32[]{:S(2)}, u32[]{:S(2)}) async-start(bf16[4,32,1856]{2,1,0:T(8,128)(2,1)} %prep.1), calls=%async_computation | async-start | bytes 983040 | tf_op jit(solution)/shard_map/all_to_all | solution.py:461
  19.1 2.3 %collective-permute-done.2.refs_4_ = bf16[8,32,512]{2,1,0:T(8,128)(2,1)S(1)} collective-permute-done((bf16[8,32,512]{2,1,0:T(8,128)(2,1)S(1)}, bf16[8,32,512]{2,1,0:T(8,128)(2,1)S(1)}, u32[]{:S(2)}, u32[]{:S(2)}) %collective-permute-start.2) | collective-permute-done | bytes 262176 | tf_op jit(solution)/shard_map/ppermute | solution.py:50
  21.4 0.7 copy-done.9
  22.1 9.4 %first.1 = (bf16[90112,384]{1,0:T(8,128)(2,1)}, f32[67584,256]{1,0:T(8,128)}) custom-call(bf16[27,4,32]{2,1,0:T(4,128)(2,1)} %bitcast.41, bf16[4,8,16,512]{3,2,1,0:T(8,128)(2,1)} %refs_1_.1, bf16[8,32,512]{2,1,0:T(8,128)(2,1)} %copy-done.8, bf16[4,8,16,512]{3,2,1,0:T(8,128)(2,1)} %collective-permute-done.1.refs_3_, bf16[8,32,512]{2,1,0:T(8,128)(2,1)} %copy-done.9, ...), custom_call_target="tpu_custom_call" | custom-call | flops 8589934592 | bytes 1048576 | tf_op jit(solution)/shard_map/first/pallas_call | solution.py:25
  31.5 1.9 %all-to-all-done = bf16[4,32,1856]{2,1,0:T(8,128)(2,1)S(1)} async-done(((bf16[4,32,1856]{2,1,0:T(8,128)(2,1)}), bf16[4,32,1856]{2,1,0:T(8,128)(2,1)S(1)}, u32[]{:S(2)}, u32[]{:S(2)}) %all-to-all-start) | async-done | bytes 475168 | tf_op jit(solution)/shard_map/all_to_all | solution.py:461
  33.5 2.0 %third.1 = (bf16[128,128]{1,0:T(8,128)(2,1)S(1)}, bf16[8,128,128]{2,1,0:T(8,128)(2,1)S(1)}, bf16[8,128,128]{2,1,0:T(8,128)(2,1)S(1)}, bf16[256,128]{1,0:T(8,128)...) custom-call(bf16[128,1856]{1,0:T(8,128)(2,1)S(1)} %bitcast.29, ...), custom_call_target="tpu_custom_call" | custom-call | flops 268435456 | bytes 1048576 | tf_op jit(solution)/shard_map/third/pallas_call | solution.py:25
  35.6 1.3 %collective-permute-start.7 = (bf16[256,128]{1,0:T(8,128)(2,1)S(1)}, bf16[256,128]{1,0:T(8,128)(2,1)S(1)}, u32[]{:S(2)}, u32[]{:S(2)}) collective-permute-start(bf16[256,128]{1,0:T(8,128)(2,1)S(1)} %get-tuple-element.29), channel_id=1, source_target_pairs={{1,0},{2,1},{3,2},{5,4},{6,5},{7,6},{9,8},{10,9},{11,10},{13,12},{... | collective-permute-start | bytes 196616 | tf_op jit(solution)/shard_map/ppermute | solution.py:44
  36.9 0.3 copy.20
  37.3 4.7 %collective-permute-done.7.rz_ref = bf16[256,128]{1,0:T(8,128)(2,1)S(1)} collective-permute-done((bf16[256,128]{1,0:T(8,128)(2,1)S(1)}, bf16[256,128]{1,0:T(8,128)(2,1)S(1)}, u32[]{:S(2)}, u32[]{:S(2)}) %collective-permute-start.7) | collective-permute-done | bytes 65568 | tf_op jit(solution)/shard_map/ppermute | solution.py:44
  42.0 1.3 %collective-permute-start.8 = (bf16[576,128]{1,0:T(8,128)(2,1)S(1)}, bf16[576,128]{1,0:T(8,128)(2,1)S(1)}, u32[]{:S(2)}, u32[]{:S(2)}) collective-permute-start(bf16[576,128]{1,0:T(8,128)(2,1)S(1)} %pad_maximum_fusion.1), channel_id=1, source_target_pairs={{4,0},{8,4},{12,8},{16,12},{20,16},{24,20},{28,24},{5,1},{9,5},{13... | collective-permute-start | bytes 442376 | tf_op jit(solution)/shard_map/ppermute | solution.py:44
  43.3 0.8 add_convert_fusion
  44.1 4.6 %all-to-all-start.1 = ((bf16[32,32,128]{2,1,0:T(8,128)(2,1)}), bf16[32,32,128]{2,1,0:T(8,128)(2,1)S(1)}, u32[]{:S(2)}, u32[]{:S(2)}) async-start(bf16[32,32,128]{2,1,0:T(8,128)(2,1)} %bitcast.10), calls=%async_computation.1 | async-start | bytes 524288 | tf_op jit(solution)/shard_map/all_to_all | solution.py:482
  48.8 6.1 %backward.1 = bf16[512,128]{1,0:T(8,128)(2,1)S(1)} custom-call(bf16[128,768]{1,0:T(8,128)(2,1)S(1)} %copy-done.4, bf16[128,128]{1,0:T(8,128)(2,1)S(1)} %get-tuple-element.28.d3_ref, bf16[256,128]{1,0:T(8,128)(2,1)S(1)} %collective-permute-done.7.rz_ref, bf16[576,128]{1,0:T(8,128)(2,1)S(1)} %collective-permute-done.8.rd_ref, ...), custom_call_target="tpu_custom_call" | custom-call | flops 68719476736 | bytes 1048576 | tf_op jit(solution)/shard_map/backward/pallas_call | solution.py:25
  54.9 4.0 %all-to-all-done.1.g3_ref = bf16[32,32,128]{2,1,0:T(8,128)(2,1)S(1)} async-done(((bf16[32,32,128]{2,1,0:T(8,128)(2,1)}), bf16[32,32,128]{2,1,0:T(8,128)(2,1)S(1)}, u32[]{:S(2)}, u32[]{:S(2)}) %all-to-all-start.1) | async-done | bytes 262176 | tf_op jit(solution)/shard_map/all_to_all | solution.py:482
  58.9 10.9 %all_to_all.20.msg_ref = bf16[32,16,128]{2,1,0:T(8,128)(2,1)S(1)} all-to-all(bf16[32,16,128]{2,1,0:T(8,128)(2,1)S(1)} %bitcast.30), channel_id=1, replica_groups=mesh['dev'=8,'ha'=4] {'dev','ha'}, dimensions={0} | all-to-all | bytes 262144 | tf_op jit(solution)/shard_map/all_to_all | solution.py:502
  69.8 0.8 sum.1
  70.6 2.6 %all-to-all-start.3 = ((bf16[32,32,128]{2,1,0:T(8,128)(2,1)}), bf16[32,32,128]{2,1,0:T(8,128)(2,1)S(1)}, u32[]{:S(2)}, u32[]{:S(2)}) async-start(bf16[32,32,128]{2,1,0:T(8,128)(2,1)} %bitcast.18), calls=%async_computation.3 | async-start | bytes 524288 | tf_op jit(solution)/shard_map/all_to_all | solution.py:505
  73.2 1.7 %collective-permute-start.3 = (bf16[32,128]{1,0:T(8,128)(2,1)S(1)}, bf16[32,128]{1,0:T(8,128)(2,1)S(1)}, u32[]{:S(2)}, u32[]{:S(2)}) collective-permute-start(bf16[32,128]{1,0:T(8,128)(2,1)S(1)} %get-tuple-element.23), channel_id=1, source_target_pairs={{0,1},{1,2},{2,3},{3,0},{4,5},{5,6},{6,7},{7,4},{8,9},{9,10},{10,1... | collective-permute-start | bytes 24584 | tf_op jit(solution)/shard_map/ppermute | solution.py:487
  74.9 2.5 %collective-permute-start.4 = (bf16[32,128]{1,0:T(8,128)(2,1)S(1)}, bf16[32,128]{1,0:T(8,128)(2,1)S(1)}, u32[]{:S(2)}, u32[]{:S(2)}) collective-permute-start(bf16[32,128]{1,0:T(8,128)(2,1)S(1)} %get-tuple-element.24), channel_id=1, source_target_pairs={{0,2},{1,3},{2,0},{3,1},{4,6},{5,7},{6,4},{7,5},{8,10},{9,11},{10,... | collective-permute-start | bytes 24584 | tf_op jit(solution)/shard_map/ppermute | solution.py:487
  77.4 1.4 %collective-permute-start.5 = (bf16[32,128]{1,0:T(8,128)(2,1)S(1)}, bf16[32,128]{1,0:T(8,128)(2,1)S(1)}, u32[]{:S(2)}, u32[]{:S(2)}) collective-permute-start(bf16[32,128]{1,0:T(8,128)(2,1)S(1)} %get-tuple-element.25), channel_id=1, source_target_pairs={{0,3},{1,0},{2,1},{3,2},{4,7},{5,4},{6,5},{7,6},{8,11},{9,8},{10,9... | collective-permute-start | bytes 24584 | tf_op jit(solution)/shard_map/ppermute | solution.py:487
  78.8 3.6 %collective-permute-done.3.refs_1_ = bf16[32,128]{1,0:T(8,128)(2,1)S(1)} collective-permute-done((bf16[32,128]{1,0:T(8,128)(2,1)S(1)}, bf16[32,128]{1,0:T(8,128)(2,1)S(1)}, u32[]{:S(2)}, u32[]{:S(2)}) %collective-permute-start.3) | collective-permute-done | bytes 8224 | tf_op jit(solution)/shard_map/ppermute | solution.py:487
  82.5 0.7 collective-permute-done.4.refs_2_
  83.2 0.1 reshape.62
  83.3 0.7 copy.19
  83.9 1.1 %unpack.1 = (f32[27,4,32]{2,1,0:T(4,128)}, f32[2,27,16,64]{3,2,1,0:T(8,128)}, f32[27,32,64]{2,1,0:T(8,128)}) custom-call(bf16[32,32,128]{2,1,0:T(8,128)(2,1)S(1)} %all-to-all-done.3.total_ref), custom_call_target="tpu_custom_call" | custom-call | flops 268435456 | bytes 1048576 | tf_op jit(solution)/shard_map/unpack/pallas_call | solution.py:25
  (30 shorter events, 0.3 us)
Async XLA Ops:
  0.6 21.4 %collective-permute-start.1 = (bf16[4,8,16,512]{3,2,1,0:T(8,128)(2,1)}, bf16[4,8,16,512]{3,2,1,0:T(8,128)(2,1)}, u32[]{:S(2)}, u32[]{:S(2)}) collective-permute-start(bf16[4,8,16,512]{3,2,1,0:T(8,128)(2,1)} %refs_1_.1), channel_id=1, source_target_pairs={{0,4},{4,8},{8,12},{12,16},{16,20},{20,24},{24,28},{1,5},{5,9},{9,... | collective-permute-start | bytes 1572872 | tf_op jit(solution)/shard_map/ppermute | solution.py:44
  4.8 14.3 %collective-permute-start = (bf16[8,32,512]{2,1,0:T(8,128)(2,1)S(1)}, bf16[8,32,512]{2,1,0:T(8,128)(2,1)S(1)}, u32[]{:S(2)}, u32[]{:S(2)}) collective-permute-start(bf16[8,32,512]{2,1,0:T(8,128)(2,1)S(1)} %copy_bitcast_fusion), channel_id=1, source_target_pairs={{0,1},{1,2},{2,3},{4,5},{5,6},{6,7},{8,9},{9,10},{10,11},{12,13},{... | collective-permute-start | bytes 786440 | tf_op jit(solution)/shard_map/ppermute | solution.py:44
  9.1 12.3 %collective-permute-start.2 = (bf16[8,32,512]{2,1,0:T(8,128)(2,1)S(1)}, bf16[8,32,512]{2,1,0:T(8,128)(2,1)S(1)}, u32[]{:S(2)}, u32[]{:S(2)}) collective-permute-start(bf16[8,32,512]{2,1,0:T(8,128)(2,1)S(1)} %copy_bitcast_fusion), channel_id=1, source_target_pairs={{0,5},{1,6},{2,7},{4,9},{5,10},{6,11},{8,13},{9,14},{10,15},{12,17... | collective-permute-start | bytes 786440 | tf_op jit(solution)/shard_map/ppermute | solution.py:50
  12.9 0.9 %copy-start = (bf16[3,3,3,64,32]{3,4,2,1,0:T(8,128)(2,1)S(1)}, bf16[3,3,3,64,32]{3,4,2,1,0:T(8,128)(2,1)}, u32[]{:S(2)}) copy-start(bf16[3,3,3,64,32]{3,4,2,1,0:T(8,128)(2,1)} %param.14) | copy-start | bytes 331780
  13.8 0.8 copy-start.2
  15.6 17.8 %all-to-all-start = ((bf16[4,32,1856]{2,1,0:T(8,128)(2,1)}), bf16[4,32,1856]{2,1,0:T(8,128)(2,1)S(1)}, u32[]{:S(2)}, u32[]{:S(2)}) async-start(bf16[4,32,1856]{2,1,0:T(8,128)(2,1)} %prep.1), calls=%async_computation | async-start | bytes 983040 | tf_op jit(solution)/shard_map/all_to_all | solution.py:461
  19.1 3.0 %copy-start.8 = (bf16[8,32,512]{2,1,0:T(8,128)(2,1)}, bf16[8,32,512]{2,1,0:T(8,128)(2,1)S(1)}, u32[]{:S(2)}) copy-start(bf16[8,32,512]{2,1,0:T(8,128)(2,1)S(1)} %collective-permute-done.refs_2_) | copy-start | bytes 786436
  21.4 0.7 copy-start.9
  33.4 15.3 %copy-start.1 = (bf16[3,3,3,32,64]{4,3,2,1,0:T(8,128)(2,1)S(1)}, bf16[3,3,3,32,64]{4,3,2,1,0:T(8,128)(2,1)}, u32[]{:S(2)}) copy-start(bf16[3,3,3,32,64]{4,3,2,1,0:T(8,128)(2,1)} %param.13) | copy-start | bytes 331780
  33.4 15.3 %copy-start.3 = (bf16[3,288,256]{2,1,0:T(8,128)(2,1)S(1)}, bf16[3,288,256]{2,1,0:T(8,128)(2,1)}, u32[]{:S(2)}) copy-start(bf16[3,288,256]{2,1,0:T(8,128)(2,1)} %constant.14.clone.mask_ref) | copy-start | bytes 1327108
  33.5 15.3 %copy-start.4 = (bf16[128,768]{1,0:T(8,128)(2,1)S(1)}, bf16[128,768]{1,0:T(8,128)(2,1)}, u32[]{:S(2)}) copy-start(bf16[128,768]{1,0:T(8,128)(2,1)} %constant.17.clone.spread_ref) | copy-start | bytes 589828
  33.5 15.3 %copy-start.5 = (bf16[256,32]{1,0:T(8,128)(2,1)S(1)}, bf16[256,32]{1,0:T(8,128)(2,1)}, u32[]{:S(2)}) copy-start(bf16[256,32]{1,0:T(8,128)(2,1)} %constant.12.clone.so_ref) | copy-start | bytes 49156
  33.5 15.3 %copy-start.6 = (bf16[128,128]{1,0:T(8,128)(2,1)S(1)}, bf16[128,128]{1,0:T(8,128)(2,1)}, u32[]{:S(2)}) copy-start(bf16[128,128]{1,0:T(8,128)(2,1)} %constant.15.clone.refs_5_.later_ref) | copy-start | bytes 98308
  33.5 15.3 %copy-start.7 = (bf16[16,288]{1,0:T(8,128)(2,1)S(1)}, bf16[16,288]{1,0:T(8,128)(2,1)}, u32[]{:S(2)}) copy-start(bf16[16,288]{1,0:T(8,128)(2,1)} %constant.13.clone.sam_ref) | copy-start | bytes 27652
  35.5 7.8 %collective-permute-start.6 = (bf16[8,128,128]{2,1,0:T(8,128)(2,1)S(1)}, bf16[8,128,128]{2,1,0:T(8,128)(2,1)S(1)}, u32[]{:S(2)}, u32[]{:S(2)}) collective-permute-start(bf16[8,128,128]{2,1,0:T(8,128)(2,1)S(1)} %get-tuple-element.27), channel_id=1, source_target_pairs={{0,4},{4,0},{8,12},{12,8},{16,20},{20,16},{24,28},{28,24},{1,5},{5... | collective-permute-start | bytes 786440 | tf_op jit(solution)/shard_map/ppermute | solution.py:480
  35.6 6.4 %collective-permute-start.7 = (bf16[256,128]{1,0:T(8,128)(2,1)S(1)}, bf16[256,128]{1,0:T(8,128)(2,1)S(1)}, u32[]{:S(2)}, u32[]{:S(2)}) collective-permute-start(bf16[256,128]{1,0:T(8,128)(2,1)S(1)} %get-tuple-element.29), channel_id=1, source_target_pairs={{1,0},{2,1},{3,2},{5,4},{6,5},{7,6},{9,8},{10,9},{11,10},{13,12},{... | collective-permute-start | bytes 196616 | tf_op jit(solution)/shard_map/ppermute | solution.py:44
  42.0 6.7 %collective-permute-start.8 = (bf16[576,128]{1,0:T(8,128)(2,1)S(1)}, bf16[576,128]{1,0:T(8,128)(2,1)S(1)}, u32[]{:S(2)}, u32[]{:S(2)}) collective-permute-start(bf16[576,128]{1,0:T(8,128)(2,1)S(1)} %pad_maximum_fusion.1), channel_id=1, source_target_pairs={{4,0},{8,4},{12,8},{16,12},{20,16},{24,20},{28,24},{5,1},{9,5},{13... | collective-permute-start | bytes 442376 | tf_op jit(solution)/shard_map/ppermute | solution.py:44
  44.1 14.8 %all-to-all-start.1 = ((bf16[32,32,128]{2,1,0:T(8,128)(2,1)}), bf16[32,32,128]{2,1,0:T(8,128)(2,1)S(1)}, u32[]{:S(2)}, u32[]{:S(2)}) async-start(bf16[32,32,128]{2,1,0:T(8,128)(2,1)} %bitcast.10), calls=%async_computation.1 | async-start | bytes 524288 | tf_op jit(solution)/shard_map/all_to_all | solution.py:482
  70.6 13.4 %all-to-all-start.3 = ((bf16[32,32,128]{2,1,0:T(8,128)(2,1)}), bf16[32,32,128]{2,1,0:T(8,128)(2,1)S(1)}, u32[]{:S(2)}, u32[]{:S(2)}) async-start(bf16[32,32,128]{2,1,0:T(8,128)(2,1)} %bitcast.18), calls=%async_computation.3 | async-start | bytes 524288 | tf_op jit(solution)/shard_map/all_to_all | solution.py:505
  73.2 9.3 %collective-permute-start.3 = (bf16[32,128]{1,0:T(8,128)(2,1)S(1)}, bf16[32,128]{1,0:T(8,128)(2,1)S(1)}, u32[]{:S(2)}, u32[]{:S(2)}) collective-permute-start(bf16[32,128]{1,0:T(8,128)(2,1)S(1)} %get-tuple-element.23), channel_id=1, source_target_pairs={{0,1},{1,2},{2,3},{3,0},{4,5},{5,6},{6,7},{7,4},{8,9},{9,10},{10,1... | collective-permute-start | bytes 24584 | tf_op jit(solution)/shard_map/ppermute | solution.py:487
  74.9 8.2 %collective-permute-start.4 = (bf16[32,128]{1,0:T(8,128)(2,1)S(1)}, bf16[32,128]{1,0:T(8,128)(2,1)S(1)}, u32[]{:S(2)}, u32[]{:S(2)}) collective-permute-start(bf16[32,128]{1,0:T(8,128)(2,1)S(1)} %get-tuple-element.24), channel_id=1, source_target_pairs={{0,2},{1,3},{2,0},{3,1},{4,6},{5,7},{6,4},{7,5},{8,10},{9,11},{10,... | collective-permute-start | bytes 24584 | tf_op jit(solution)/shard_map/ppermute | solution.py:487
  77.4 5.7 %collective-permute-start.5 = (bf16[32,128]{1,0:T(8,128)(2,1)S(1)}, bf16[32,128]{1,0:T(8,128)(2,1)S(1)}, u32[]{:S(2)}, u32[]{:S(2)}) collective-permute-start(bf16[32,128]{1,0:T(8,128)(2,1)S(1)} %get-tuple-element.25), channel_id=1, source_target_pairs={{0,3},{1,0},{2,1},{3,2},{4,7},{5,4},{6,5},{7,6},{8,11},{9,8},{10,9... | collective-permute-start | bytes 24584 | tf_op jit(solution)/shard_map/ppermute | solution.py:487

commit v3 on v2

--- a/solution.py
+++ b/solution.py
@@ -113,10 +113,10 @@
 
 def deinterleave(width):
     s = width // 8
-    col = lax.broadcasted_iota(jnp.int32, (1, 12 * s), 1)
+    col = lax.broadcasted_iota(jnp.int32, (1, 8 * s), 1)
     k = col % (4 * s) // s
-    source = 8 * (col % s) + 2 * (k % 2 * 2 + k // 2) - 1 + col // (4 * s)
-    row = lax.broadcasted_iota(jnp.int32, (width, 12 * s), 0)
+    source = 8 * (col % s) + 2 * (k % 2 * 2 + k // 2) + col // (4 * s)
+    row = lax.broadcasted_iota(jnp.int32, (width, 8 * s), 0)
     return jnp.where(row == source, 1.0, 0.0).astype(BF)
 
 
@@ -172,23 +172,27 @@
     for j in range(11):
         part = mm(wt, taps[j])
         t_ref[j * 32:j * 32 + 32] = jnp.concatenate([part[0:32], part[32:64], part[64:96]], 1).astype(BF)
+    fetches[5].wait()
+    later = later_ref[...]
     for volume, edges, first, skip, given in ((volume_ref, hz_ref, 7, 0, (1, 2)), (dd_ref, dz_ref, -1, 1, (3, 4))):
         for i in given:
             fetches[i].wait()
         side = mm(edges[...].reshape(256, -1), sel).astype(BF)
         main = [mm(volume[m, skip:].reshape((8 - skip) * 16, -1), sel).astype(BF) for m in range(4)]
+        parts = [(part, mm(part[:, 384:512], later).astype(BF)) for part in (*main, side)]
         for d in range(skip, 8):
             base = (first + d) * 96
-            for e in range(3):
-                lanes = slice(e * 256, e * 256 + 256)
-                for m in range(4):
-                    x1_ref[e, base + m * 16:base + m * 16 + 16] = main[m][(d - skip) * 16:(d - skip) * 16 + 16, lanes]
-                x1_ref[e, base + 64:base + 96] = side[d * 32:d * 32 + 32, lanes]
+            for m, (part, moved) in enumerate(parts):
+                size = 16 if m < 4 else 32
+                rows = slice(d * 32, d * 32 + 32) if m == 4 else slice((d - skip) * 16, (d - skip) * 16 + 16)
+                here = slice(base + m * 16, base + m * 16 + size)
+                x1_ref[1, here] = part[rows, 0:256]
+                x1_ref[2, here] = part[rows, 256:512]
+                x1_ref[0, here, 0:128] = moved[rows]
+                x1_ref[0, here, 128:256] = part[rows, 256:384]
     for e in range(3):
         send(x1_ref.at[e, 576:1440], park_b, "x1", e * 864)
     t = t_ref[...]
-    fetches[5].wait()
-    later = later_ref[...]
     for ii in range(7):
         lo = ii * 192
         z = mm(t, jnp.concatenate([x1_ref[e, lo:lo + 288] for e in range(3)], 0))
@@ -452,12 +456,13 @@
 
     edge = volume[:, :, 8:].transpose(1, 0, 2, 3).reshape(8, 32, width)
     dd = shifted(volume, "dev", 1)
-    dz = diagonal(edge)
     hz = shifted(edge, "ha", 1)
 
     ch = 128 // nh
     natural = w_third.transpose(0, 1, 2, 4, 3).reshape(27, ch, 64)
     both, = call("prep", prep_body, [cotangent[:, 0], natural], [], [array(BF, nh, ch, 1856)], limit=8)
+    hz, both = lax.optimization_barrier((hz, both))
+    dz = shifted(hz, "dev", 1)
     both = lax.all_to_all(both, "ha", 0, 0, tiled=True).reshape(128, 1856)
     w2 = w_second.reshape(864, 64)
     dma = pltpu.SemaphoreType.DMA

time: 85.6 us -> 85.4 us (level)
    ppermute x1 -> x0, starting transfers between devices: 3.8 us -> none  [diagonal(): return lax.ppermute(block, ('dev', 'ha'), route)]
    ppermute x4 -> x5, starting transfers between devices: 10.1 us -> 12.4 us  [shifted(): return lax.ppermute(block, axis, route)]
    all_to_all x1, waiting for transfers between devices: 1.89 us -> 4.2 us  [local(): both = lax.all_to_all(both, 'ha', 0, 0, tiled=True).reshape(128, 1856)]
    ppermute x1 -> x0, waiting for transfers between devices: 2.26 us -> none  [diagonal(): return lax.ppermute(block, ('dev', 'ha'), route)]
    all_to_all x1, starting transfers between devices: 3.47 us -> 4.47 us  [local(): both = lax.all_to_all(both, 'ha', 0, 0, tiled=True).reshape(128, 1856)]
    ppermute x4 -> x5, waiting for transfers between devices: 4.71 us -> 5.06 us  [shifted(): return lax.ppermute(block, axis, route)]
  transfers between devices with their start and end apart: 12 -> 12, of which waited for: 6 -> 6; matrix products, arithmetic and copies ran while one was open for 3% -> 2% of each run, Pallas kernels for 19% -> 19%
where the time goes in v3:
time: 85.4 us; the launch traced here: 84.8 us
  starting transfers between devices  29.7 us (35%)
  Pallas kernels  20.3 us (24%)
  waiting for transfers between devices  17.6 us (21%)
  blocking collectives  10.9 us (13%)
  local copies, waits for them, and re-layouts  4.59 us (5%)
  between operations  0.87 us (1%)
    pallas_call x7, Pallas kernels, call(): pl.pallas_call(body, out_shape=(*outputs, *far_outputs), in_specs=[near]...  20.3 us
    ppermute x5, starting transfers between devices, shifted(): return lax.ppermute(block, axis, route)  12.4 us
    all_to_all x1, blocking collectives, local(): lax.all_to_all(msg.reshape(n, 512 // n, 128), ('dev', 'ha'), 0, 0, tiled=...  10.9 us
    ppermute x3, starting transfers between devices, local(): lax.ppermute(blocks[k], 'ha', [(i, (i + k) % nh) for i in range(nh)])  5.63 us
    ppermute x5, waiting for transfers between devices, shifted(): return lax.ppermute(block, axis, route)  5.06 us
    all_to_all x1, starting transfers between devices, local(): both = lax.all_to_all(both, 'ha', 0, 0, tiled=True).reshape(128, 1856)  4.47 us
    ppermute x3, waiting for transfers between devices, local(): lax.ppermute(blocks[k], 'ha', [(i, (i + k) % nh) for i in range(nh)])  4.35 us
    all_to_all x1, waiting for transfers between devices, local(): both = lax.all_to_all(both, 'ha', 0, 0, tiled=True).reshape(128, 1856)  4.2 us
  transfers between devices with their start and end apart: 12, of which 6 were waited for; matrix products, arithmetic and copies ran while one was open for 2% of the time, Pallas kernels for 19%

profile of v3, /device:TPU:0, one launch (start us, length us, event | category | flops | bytes accessed | tf_op | source)
XLA Modules:
  0.0 84.8 jit_solution(50024776253992110)
XLA Ops:
  0.6 1.0 %copy_bitcast_fusion = bf16[8,32,512]{2,1,0:T(8,128)(2,1)S(1)} fusion(bf16[4,8,16,512]{3,2,1,0:T(8,128)(2,1)} %refs_1_.1), kind=kLoop, calls=%fused_computation.2 | loop fusion | bytes 524288 | tf_op jit(solution)/shard_map/reshape | solution.py:457
  1.6 4.9 %collective-permute-start = (bf16[8,32,512]{2,1,0:T(8,128)(2,1)S(1)}, bf16[8,32,512]{2,1,0:T(8,128)(2,1)S(1)}, u32[]{:S(2)}, u32[]{:S(2)}) collective-permute-start(bf16[8,32,512]{2,1,0:T(8,128)(2,1)S(1)} %copy_bitcast_fusion), channel_id=1, source_target_pairs={{0,1},{1,2},{2,3},{4,5},{5,6},{6,7},{8,9},{9,10},{10,11},{12,13},{... | collective-permute-start | bytes 786440 | tf_op jit(solution)/shard_map/ppermute | solution.py:44
  6.6 2.3 %collective-permute-start.1 = (bf16[4,8,16,512]{3,2,1,0:T(8,128)(2,1)}, bf16[4,8,16,512]{3,2,1,0:T(8,128)(2,1)}, u32[]{:S(2)}, u32[]{:S(2)}) collective-permute-start(bf16[4,8,16,512]{3,2,1,0:T(8,128)(2,1)} %refs_1_.1), channel_id=1, source_target_pairs={{0,4},{4,8},{8,12},{12,16},{16,20},{20,24},{24,28},{1,5},{5,9},{9,... | collective-permute-start | bytes 1572872 | tf_op jit(solution)/shard_map/ppermute | solution.py:44
  8.8 0.9 %copy-done = bf16[3,3,3,64,32]{3,4,2,1,0:T(8,128)(2,1)S(1)} copy-done((bf16[3,3,3,64,32]{3,4,2,1,0:T(8,128)(2,1)S(1)}, bf16[3,3,3,64,32]{3,4,2,1,0:T(8,128)(2,1)}, u32[]{:S(2)}) %copy-start) | copy-done | bytes 110616
  9.8 0.8 copy-done.2
  10.6 0.9 %prep.1 = bf16[4,32,1856]{2,1,0:T(8,128)(2,1)} custom-call(bf16[32,8,64]{2,1,0:T(8,128)(2,1)S(1)} %bitcast.34, bf16[27,32,64]{2,1,0:T(8,128)(2,1)S(1)} %bitcast.31), custom_call_target="tpu_custom_call" | custom-call | flops 268435456 | bytes 1048576 | tf_op jit(solution)/shard_map/prep/pallas_call | solution.py:25
  11.5 0.6 collective-permute-done.refs_2_
  12.1 2.6 %collective-permute-start.2 = (bf16[8,32,512]{2,1,0:T(8,128)(2,1)S(1)}, bf16[8,32,512]{2,1,0:T(8,128)(2,1)S(1)}, u32[]{:S(2)}, u32[]{:S(2)}) collective-permute-start(bf16[8,32,512]{2,1,0:T(8,128)(2,1)S(1)} %collective-permute-done.refs_2_), channel_id=1, source_target_pairs={{0,4},{4,8},{8,12},{12,16},{16,20},{20,24},{24,28},{1,5},{5,9},{9,... | collective-permute-start | bytes 786440 | tf_op jit(solution)/shard_map/ppermute | solution.py:44
  14.7 4.5 %all-to-all-start = ((bf16[4,32,1856]{2,1,0:T(8,128)(2,1)}), bf16[4,32,1856]{2,1,0:T(8,128)(2,1)S(1)}, u32[]{:S(2)}, u32[]{:S(2)}) async-start(bf16[4,32,1856]{2,1,0:T(8,128)(2,1)} %prep.1), calls=%async_computation | async-start | bytes 983040 | tf_op jit(solution)/shard_map/all_to_all | solution.py:466
  19.2 0.7 copy-done.9
  19.9 9.3 %first.1 = (bf16[90112,384]{1,0:T(8,128)(2,1)}, f32[67584,256]{1,0:T(8,128)}) custom-call(bf16[27,4,32]{2,1,0:T(4,128)(2,1)} %bitcast.41, bf16[4,8,16,512]{3,2,1,0:T(8,128)(2,1)} %refs_1_.1, bf16[8,32,512]{2,1,0:T(8,128)(2,1)} %copy-done.8, bf16[4,8,16,512]{3,2,1,0:T(8,128)(2,1)} %collective-permute-done.1.refs_3_, bf16[8,32,512]{2,1,0:T(8,128)(2,1)} %copy-done.9, ...), custom_call_target="tpu_custom_call" | custom-call | flops 8589934592 | bytes 1048576 | tf_op jit(solution)/shard_map/first/pallas_call | solution.py:25
  29.2 4.2 %all-to-all-done = bf16[4,32,1856]{2,1,0:T(8,128)(2,1)S(1)} async-done(((bf16[4,32,1856]{2,1,0:T(8,128)(2,1)}), bf16[4,32,1856]{2,1,0:T(8,128)(2,1)S(1)}, u32[]{:S(2)}, u32[]{:S(2)}) %all-to-all-start) | async-done | bytes 475168 | tf_op jit(solution)/shard_map/all_to_all | solution.py:466
  33.5 2.0 %third.1 = (bf16[128,128]{1,0:T(8,128)(2,1)S(1)}, bf16[8,128,128]{2,1,0:T(8,128)(2,1)S(1)}, bf16[8,128,128]{2,1,0:T(8,128)(2,1)S(1)}, bf16[256,128]{1,0:T(8,128)...) custom-call(bf16[128,1856]{1,0:T(8,128)(2,1)S(1)} %bitcast.29, ...), custom_call_target="tpu_custom_call" | custom-call | flops 268435456 | bytes 1048576 | tf_op jit(solution)/shard_map/third/pallas_call | solution.py:25
  35.6 0.8 collective-permute-start.6
  36.4 1.3 %collective-permute-start.7 = (bf16[256,128]{1,0:T(8,128)(2,1)S(1)}, bf16[256,128]{1,0:T(8,128)(2,1)S(1)}, u32[]{:S(2)}, u32[]{:S(2)}) collective-permute-start(bf16[256,128]{1,0:T(8,128)(2,1)S(1)} %get-tuple-element.33), channel_id=1, source_target_pairs={{1,0},{2,1},{3,2},{5,4},{6,5},{7,6},{9,8},{10,9},{11,10},{13,12},{... | collective-permute-start | bytes 196616 | tf_op jit(solution)/shard_map/ppermute | solution.py:44
  37.7 0.3 copy.20
  38.1 4.5 %collective-permute-done.7.rz_ref = bf16[256,128]{1,0:T(8,128)(2,1)S(1)} collective-permute-done((bf16[256,128]{1,0:T(8,128)(2,1)S(1)}, bf16[256,128]{1,0:T(8,128)(2,1)S(1)}, u32[]{:S(2)}, u32[]{:S(2)}) %collective-permute-start.7) | collective-permute-done | bytes 65568 | tf_op jit(solution)/shard_map/ppermute | solution.py:44
  42.6 1.3 %collective-permute-start.8 = (bf16[576,128]{1,0:T(8,128)(2,1)S(1)}, bf16[576,128]{1,0:T(8,128)(2,1)S(1)}, u32[]{:S(2)}, u32[]{:S(2)}) collective-permute-start(bf16[576,128]{1,0:T(8,128)(2,1)S(1)} %pad_maximum_fusion.1), channel_id=1, source_target_pairs={{4,0},{8,4},{12,8},{16,12},{20,16},{24,20},{28,24},{5,1},{9,5},{13... | collective-permute-start | bytes 442376 | tf_op jit(solution)/shard_map/ppermute | solution.py:44
  43.9 0.8 add_convert_fusion
  44.7 3.8 %all-to-all-start.1 = ((bf16[32,32,128]{2,1,0:T(8,128)(2,1)}), bf16[32,32,128]{2,1,0:T(8,128)(2,1)S(1)}, u32[]{:S(2)}, u32[]{:S(2)}) async-start(bf16[32,32,128]{2,1,0:T(8,128)(2,1)} %bitcast.10), calls=%async_computation.1 | async-start | bytes 524288 | tf_op jit(solution)/shard_map/all_to_all | solution.py:487
  48.5 6.2 %backward.1 = bf16[512,128]{1,0:T(8,128)(2,1)S(1)} custom-call(bf16[128,768]{1,0:T(8,128)(2,1)S(1)} %copy-done.4, bf16[128,128]{1,0:T(8,128)(2,1)S(1)} %get-tuple-element.32.d3_ref, bf16[256,128]{1,0:T(8,128)(2,1)S(1)} %collective-permute-done.7.rz_ref, bf16[576,128]{1,0:T(8,128)(2,1)S(1)} %collective-permute-done.8.rd_ref, ...), custom_call_target="tpu_custom_call" | custom-call | flops 68719476736 | bytes 1048576 | tf_op jit(solution)/shard_map/backward/pallas_call | solution.py:25
  54.7 4.0 %all-to-all-done.1.g3_ref = bf16[32,32,128]{2,1,0:T(8,128)(2,1)S(1)} async-done(((bf16[32,32,128]{2,1,0:T(8,128)(2,1)}), bf16[32,32,128]{2,1,0:T(8,128)(2,1)S(1)}, u32[]{:S(2)}, u32[]{:S(2)}) %all-to-all-start.1) | async-done | bytes 262176 | tf_op jit(solution)/shard_map/all_to_all | solution.py:487
  58.7 10.9 %all_to_all.20.msg_ref = bf16[32,16,128]{2,1,0:T(8,128)(2,1)S(1)} all-to-all(bf16[32,16,128]{2,1,0:T(8,128)(2,1)S(1)} %bitcast.30), channel_id=1, replica_groups=mesh['dev'=8,'ha'=4] {'dev','ha'}, dimensions={0} | all-to-all | bytes 262144 | tf_op jit(solution)/shard_map/all_to_all | solution.py:507
  69.6 0.8 sum.1
  70.4 2.6 %all-to-all-start.3 = ((bf16[32,32,128]{2,1,0:T(8,128)(2,1)}), bf16[32,32,128]{2,1,0:T(8,128)(2,1)S(1)}, u32[]{:S(2)}, u32[]{:S(2)}) async-start(bf16[32,32,128]{2,1,0:T(8,128)(2,1)} %bitcast.18), calls=%async_computation.3 | async-start | bytes 524288 | tf_op jit(solution)/shard_map/all_to_all | solution.py:510
  72.9 1.7 %collective-permute-start.3 = (bf16[32,128]{1,0:T(8,128)(2,1)S(1)}, bf16[32,128]{1,0:T(8,128)(2,1)S(1)}, u32[]{:S(2)}, u32[]{:S(2)}) collective-permute-start(bf16[32,128]{1,0:T(8,128)(2,1)S(1)} %get-tuple-element.27), channel_id=1, source_target_pairs={{0,1},{1,2},{2,3},{3,0},{4,5},{5,6},{6,7},{7,4},{8,9},{9,10},{10,1... | collective-permute-start | bytes 24584 | tf_op jit(solution)/shard_map/ppermute | solution.py:492
  74.7 2.5 %collective-permute-start.4 = (bf16[32,128]{1,0:T(8,128)(2,1)S(1)}, bf16[32,128]{1,0:T(8,128)(2,1)S(1)}, u32[]{:S(2)}, u32[]{:S(2)}) collective-permute-start(bf16[32,128]{1,0:T(8,128)(2,1)S(1)} %get-tuple-element.28), channel_id=1, source_target_pairs={{0,2},{1,3},{2,0},{3,1},{4,6},{5,7},{6,4},{7,5},{8,10},{9,11},{10,... | collective-permute-start | bytes 24584 | tf_op jit(solution)/shard_map/ppermute | solution.py:492
  77.2 1.4 %collective-permute-start.5 = (bf16[32,128]{1,0:T(8,128)(2,1)S(1)}, bf16[32,128]{1,0:T(8,128)(2,1)S(1)}, u32[]{:S(2)}, u32[]{:S(2)}) collective-permute-start(bf16[32,128]{1,0:T(8,128)(2,1)S(1)} %get-tuple-element.29), channel_id=1, source_target_pairs={{0,3},{1,0},{2,1},{3,2},{4,7},{5,4},{6,5},{7,6},{8,11},{9,8},{10,9... | collective-permute-start | bytes 24584 | tf_op jit(solution)/shard_map/ppermute | solution.py:492
  78.6 3.6 %collective-permute-done.3.refs_1_ = bf16[32,128]{1,0:T(8,128)(2,1)S(1)} collective-permute-done((bf16[32,128]{1,0:T(8,128)(2,1)S(1)}, bf16[32,128]{1,0:T(8,128)(2,1)S(1)}, u32[]{:S(2)}, u32[]{:S(2)}) %collective-permute-start.3) | collective-permute-done | bytes 8224 | tf_op jit(solution)/shard_map/ppermute | solution.py:492
  82.2 0.7 collective-permute-done.4.refs_2_
  83.0 0.7 copy.19
  83.7 1.1 %unpack.1 = (f32[27,4,32]{2,1,0:T(4,128)}, f32[2,27,16,64]{3,2,1,0:T(8,128)}, f32[27,32,64]{2,1,0:T(8,128)}) custom-call(bf16[32,32,128]{2,1,0:T(8,128)(2,1)S(1)} %all-to-all-done.3.total_ref), custom_call_target="tpu_custom_call" | custom-call | flops 268435456 | bytes 1048576 | tf_op jit(solution)/shard_map/unpack/pallas_call | solution.py:25
  (30 shorter events, 0.3 us)
Async XLA Ops:
  1.6 10.5 %collective-permute-start = (bf16[8,32,512]{2,1,0:T(8,128)(2,1)S(1)}, bf16[8,32,512]{2,1,0:T(8,128)(2,1)S(1)}, u32[]{:S(2)}, u32[]{:S(2)}) collective-permute-start(bf16[8,32,512]{2,1,0:T(8,128)(2,1)S(1)} %copy_bitcast_fusion), channel_id=1, source_target_pairs={{0,1},{1,2},{2,3},{4,5},{5,6},{6,7},{8,9},{9,10},{10,11},{12,13},{... | collective-permute-start | bytes 786440 | tf_op jit(solution)/shard_map/ppermute | solution.py:44
  6.6 12.6 %collective-permute-start.1 = (bf16[4,8,16,512]{3,2,1,0:T(8,128)(2,1)}, bf16[4,8,16,512]{3,2,1,0:T(8,128)(2,1)}, u32[]{:S(2)}, u32[]{:S(2)}) collective-permute-start(bf16[4,8,16,512]{3,2,1,0:T(8,128)(2,1)} %refs_1_.1), channel_id=1, source_target_pairs={{0,4},{4,8},{8,12},{12,16},{16,20},{20,24},{24,28},{1,5},{5,9},{9,... | collective-permute-start | bytes 1572872 | tf_op jit(solution)/shard_map/ppermute | solution.py:44
  8.8 0.9 %copy-start = (bf16[3,3,3,64,32]{3,4,2,1,0:T(8,128)(2,1)S(1)}, bf16[3,3,3,64,32]{3,4,2,1,0:T(8,128)(2,1)}, u32[]{:S(2)}) copy-start(bf16[3,3,3,64,32]{3,4,2,1,0:T(8,128)(2,1)} %param.14) | copy-start | bytes 331780
  9.8 0.8 copy-start.2
  12.1 7.8 %copy-start.8 = (bf16[8,32,512]{2,1,0:T(8,128)(2,1)}, bf16[8,32,512]{2,1,0:T(8,128)(2,1)S(1)}, u32[]{:S(2)}) copy-start(bf16[8,32,512]{2,1,0:T(8,128)(2,1)S(1)} %collective-permute-done.refs_2_) | copy-start | bytes 786436
  12.1 7.1 %collective-permute-start.2 = (bf16[8,32,512]{2,1,0:T(8,128)(2,1)S(1)}, bf16[8,32,512]{2,1,0:T(8,128)(2,1)S(1)}, u32[]{:S(2)}, u32[]{:S(2)}) collective-permute-start(bf16[8,32,512]{2,1,0:T(8,128)(2,1)S(1)} %collective-permute-done.refs_2_), channel_id=1, source_target_pairs={{0,4},{4,8},{8,12},{12,16},{16,20},{20,24},{24,28},{1,5},{5,9},{9,... | collective-permute-start | bytes 786440 | tf_op jit(solution)/shard_map/ppermute | solution.py:44
  14.7 18.7 %all-to-all-start = ((bf16[4,32,1856]{2,1,0:T(8,128)(2,1)}), bf16[4,32,1856]{2,1,0:T(8,128)(2,1)S(1)}, u32[]{:S(2)}, u32[]{:S(2)}) async-start(bf16[4,32,1856]{2,1,0:T(8,128)(2,1)} %prep.1), calls=%async_computation | async-start | bytes 983040 | tf_op jit(solution)/shard_map/all_to_all | solution.py:466
  19.2 0.7 copy-start.9
  33.5 15.0 %copy-start.1 = (bf16[3,3,3,32,64]{4,3,2,1,0:T(8,128)(2,1)S(1)}, bf16[3,3,3,32,64]{4,3,2,1,0:T(8,128)(2,1)}, u32[]{:S(2)}) copy-start(bf16[3,3,3,32,64]{4,3,2,1,0:T(8,128)(2,1)} %param.13) | copy-start | bytes 331780
  33.5 15.0 %copy-start.3 = (bf16[3,288,256]{2,1,0:T(8,128)(2,1)S(1)}, bf16[3,288,256]{2,1,0:T(8,128)(2,1)}, u32[]{:S(2)}) copy-start(bf16[3,288,256]{2,1,0:T(8,128)(2,1)} %constant.14.clone.mask_ref) | copy-start | bytes 1327108
  33.5 15.0 %copy-start.4 = (bf16[128,768]{1,0:T(8,128)(2,1)S(1)}, bf16[128,768]{1,0:T(8,128)(2,1)}, u32[]{:S(2)}) copy-start(bf16[128,768]{1,0:T(8,128)(2,1)} %constant.17.clone.spread_ref) | copy-start | bytes 589828
  33.5 15.0 %copy-start.5 = (bf16[256,32]{1,0:T(8,128)(2,1)S(1)}, bf16[256,32]{1,0:T(8,128)(2,1)}, u32[]{:S(2)}) copy-start(bf16[256,32]{1,0:T(8,128)(2,1)} %constant.12.clone.so_ref) | copy-start | bytes 49156
  33.5 15.0 %copy-start.6 = (bf16[128,128]{1,0:T(8,128)(2,1)S(1)}, bf16[128,128]{1,0:T(8,128)(2,1)}, u32[]{:S(2)}) copy-start(bf16[128,128]{1,0:T(8,128)(2,1)} %constant.15.clone.refs_5_.later_ref) | copy-start | bytes 98308
  33.5 15.0 %copy-start.7 = (bf16[16,288]{1,0:T(8,128)(2,1)S(1)}, bf16[16,288]{1,0:T(8,128)(2,1)}, u32[]{:S(2)}) copy-start(bf16[16,288]{1,0:T(8,128)(2,1)} %constant.13.clone.sam_ref) | copy-start | bytes 27652
  35.6 8.3 %collective-permute-start.6 = (bf16[8,128,128]{2,1,0:T(8,128)(2,1)S(1)}, bf16[8,128,128]{2,1,0:T(8,128)(2,1)S(1)}, u32[]{:S(2)}, u32[]{:S(2)}) collective-permute-start(bf16[8,128,128]{2,1,0:T(8,128)(2,1)S(1)} %get-tuple-element.31), channel_id=1, source_target_pairs={{0,4},{4,0},{8,12},{12,8},{16,20},{20,16},{24,28},{28,24},{1,5},{5... | collective-permute-start | bytes 786440 | tf_op jit(solution)/shard_map/ppermute | solution.py:485
  36.4 6.1 %collective-permute-start.7 = (bf16[256,128]{1,0:T(8,128)(2,1)S(1)}, bf16[256,128]{1,0:T(8,128)(2,1)S(1)}, u32[]{:S(2)}, u32[]{:S(2)}) collective-permute-start(bf16[256,128]{1,0:T(8,128)(2,1)S(1)} %get-tuple-element.33), channel_id=1, source_target_pairs={{1,0},{2,1},{3,2},{5,4},{6,5},{7,6},{9,8},{10,9},{11,10},{13,12},{... | collective-permute-start | bytes 196616 | tf_op jit(solution)/shard_map/ppermute | solution.py:44
  42.6 5.9 %collective-permute-start.8 = (bf16[576,128]{1,0:T(8,128)(2,1)S(1)}, bf16[576,128]{1,0:T(8,128)(2,1)S(1)}, u32[]{:S(2)}, u32[]{:S(2)}) collective-permute-start(bf16[576,128]{1,0:T(8,128)(2,1)S(1)} %pad_maximum_fusion.1), channel_id=1, source_target_pairs={{4,0},{8,4},{12,8},{16,12},{20,16},{24,20},{28,24},{5,1},{9,5},{13... | collective-permute-start | bytes 442376 | tf_op jit(solution)/shard_map/ppermute | solution.py:44
  44.7 14.0 %all-to-all-start.1 = ((bf16[32,32,128]{2,1,0:T(8,128)(2,1)}), bf16[32,32,128]{2,1,0:T(8,128)(2,1)S(1)}, u32[]{:S(2)}, u32[]{:S(2)}) async-start(bf16[32,32,128]{2,1,0:T(8,128)(2,1)} %bitcast.10), calls=%async_computation.1 | async-start | bytes 524288 | tf_op jit(solution)/shard_map/all_to_all | solution.py:487
  70.4 13.4 %all-to-all-start.3 = ((bf16[32,32,128]{2,1,0:T(8,128)(2,1)}), bf16[32,32,128]{2,1,0:T(8,128)(2,1)S(1)}, u32[]{:S(2)}, u32[]{:S(2)}) async-start(bf16[32,32,128]{2,1,0:T(8,128)(2,1)} %bitcast.18), calls=%async_computation.3 | async-start | bytes 524288 | tf_op jit(solution)/shard_map/all_to_all | solution.py:510
  72.9 9.3 %collective-permute-start.3 = (bf16[32,128]{1,0:T(8,128)(2,1)S(1)}, bf16[32,128]{1,0:T(8,128)(2,1)S(1)}, u32[]{:S(2)}, u32[]{:S(2)}) collective-permute-start(bf16[32,128]{1,0:T(8,128)(2,1)S(1)} %get-tuple-element.27), channel_id=1, source_target_pairs={{0,1},{1,2},{2,3},{3,0},{4,5},{5,6},{6,7},{7,4},{8,9},{9,10},{10,1... | collective-permute-start | bytes 24584 | tf_op jit(solution)/shard_map/ppermute | solution.py:492
  74.7 8.2 %collective-permute-start.4 = (bf16[32,128]{1,0:T(8,128)(2,1)S(1)}, bf16[32,128]{1,0:T(8,128)(2,1)S(1)}, u32[]{:S(2)}, u32[]{:S(2)}) collective-permute-start(bf16[32,128]{1,0:T(8,128)(2,1)S(1)} %get-tuple-element.28), channel_id=1, source_target_pairs={{0,2},{1,3},{2,0},{3,1},{4,6},{5,7},{6,4},{7,5},{8,10},{9,11},{10,... | collective-permute-start | bytes 24584 | tf_op jit(solution)/shard_map/ppermute | solution.py:492
  77.2 5.7 %collective-permute-start.5 = (bf16[32,128]{1,0:T(8,128)(2,1)S(1)}, bf16[32,128]{1,0:T(8,128)(2,1)S(1)}, u32[]{:S(2)}, u32[]{:S(2)}) collective-permute-start(bf16[32,128]{1,0:T(8,128)(2,1)S(1)} %get-tuple-element.29), channel_id=1, source_target_pairs={{0,3},{1,0},{2,1},{3,2},{4,7},{5,4},{6,5},{7,6},{8,11},{9,8},{10,9... | collective-permute-start | bytes 24584 | tf_op jit(solution)/shard_map/ppermute | solution.py:492

commit v4 on v2

--- a/solution.py
+++ b/solution.py
@@ -245,8 +245,8 @@
         copy.wait()
 
 
-def third_body(g3_slices, both_ref, park_b, park_f, d3_ref, kept_ref, given_ref, sz_ref, sd_ref, *refs):
-    blocks, (x3_ref, slope2_ref, out_ref, g3_ref, sems) = refs[:-5], refs[-5:]
+def third_body(both_ref, park_b, park_f, d3_ref, sz_ref, sd_ref, *refs):
+    blocks, (x3_ref, slope2_ref, out_ref, sems) = refs[:-4], refs[-4:]
     fetches = (
         pltpu.make_async_copy(parked(park_b, "x3", 128), x3_ref, sems.at[0]),
         pltpu.make_async_copy(parked(park_f, "slope2", 128), slope2_ref, sems.at[1]),
@@ -269,12 +269,20 @@
     for p in range(2):
         sz_ref[128 + 64 * p:192 + 64 * p] = slope2_ref[256 * p:256 * p + 64].astype(BF)
     sd_ref[128:384] = slope2_ref[0:256].astype(BF)
+
+
+def third_grad_body(g3_slices, nh, d3_ref, park_b, kept_ref, given_ref, x3_ref, g3_ref, sems):
+    fetch = pltpu.make_async_copy(parked(park_b, "x3", 128), x3_ref, sems.at[0])
+    fetch.start()
+    ch = 128 // nh
+    d3 = d3_ref[...]
     slices = 128 // g3_slices
     row = lax.broadcasted_iota(jnp.int32, (128, 1), 0)
     source = row // slices % nh * ch + row // (nh * slices) * slices + row % slices
     order = jnp.where(lax.broadcasted_iota(jnp.int32, (128, 128), 1) == source, 1.0, 0.0).astype(BF)
     ordered = mm(order, d3).astype(BF)
-    wide = jnp.concatenate([x3, jnp.zeros((64, 128), BF)], 0)
+    fetch.wait()
+    wide = jnp.concatenate([x3_ref[...], jnp.zeros((64, 128), BF)], 0)
     g3 = mm_nt(ordered, wide).astype(BF)
     for k in range(14):
         g3_ref[k] = g3[:, k * 128:k * 128 + 128]
@@ -472,10 +480,14 @@
         63, 1 << 33)
 
     n = nd * nh
-    d3, kept, given, sz, sd, *blocks = call(
-        "third", functools.partial(third_body, nh * (n // 8)), [both], [park_b, park_f],
-        [array(BF, 128, 128), array(BF, 8, 128, 128), array(BF, 8, 128, 128), array(BF, 256, 128), array(BF, 384, 128), *[array(BF, ch, 128)] * nh],
-        (), [vmem((1728, 128), BF), vmem((512, 128), F32), vmem((128, 128), F32), vmem((16, 128, 128), BF), dma((2,))], 8)
+    d3, sz, sd, *blocks = call(
+        "third", third_body, [both], [park_b, park_f],
+        [array(BF, 128, 128), array(BF, 256, 128), array(BF, 384, 128), *[array(BF, ch, 128)] * nh],
+        (), [vmem((1728, 128), BF), vmem((512, 128), F32), vmem((128, 128), F32), dma((2,))], 8)
+    kept, given = call(
+        "third_grad", functools.partial(third_grad_body, nh * (n // 8), nh), [d3], [park_b],
+        [array(BF, 8, 128, 128), array(BF, 8, 128, 128)],
+        (), [vmem((1728, 128), BF), vmem((16, 128, 128), BF), dma((1,))], 8, 1 << 32)
 
     given = lax.ppermute(given, "dev", [(i, i ^ 1) for i in range(nd)])
     halves = (kept.astype(F32) + given.astype(F32)).astype(BF)

time: 85.6 us -> 84.8 us (level)
  waiting for transfers between devices: 17.2 us -> 15.4 us
  Pallas kernels: 20.4 us -> 21.3 us
    ppermute x4, waiting for transfers between devices: 4.71 us -> 2.97 us  [shifted(): return lax.ppermute(block, axis, route)]
    pallas_call x7 -> x8, Pallas kernels: 20.4 us -> 21.3 us  [call(): pl.pallas_call(body, out_shape=(*outputs, *far_outputs), in_specs=[near]...]
  transfers between devices with their start and end apart: 12 -> 12, of which waited for: 6 -> 6; matrix products, arithmetic and copies ran while one was open for 3% -> 3% of each run, Pallas kernels for 19% -> 21%
where the time goes in v4:
time: 84.8 us; the launch traced here: 84.3 us
  starting transfers between devices  30.3 us (36%)
  Pallas kernels  21.3 us (25%)
  waiting for transfers between devices  15.4 us (18%)
  blocking collectives  10.9 us (13%)
  local copies, waits for them, and re-layouts  4.58 us (5%)
  between operations  0.91 us (1%)
  other arithmetic  0.85 us (1%)
    pallas_call x8, Pallas kernels, call(): pl.pallas_call(body, out_shape=(*outputs, *far_outputs), in_specs=[near]...  21.3 us
    all_to_all x1, blocking collectives, local(): lax.all_to_all(msg.reshape(n, 512 // n, 128), ('dev', 'ha'), 0, 0, tiled=...  10.9 us
    ppermute x4, starting transfers between devices, shifted(): return lax.ppermute(block, axis, route)  10.2 us
    ppermute x3, starting transfers between devices, local(): lax.ppermute(blocks[k], 'ha', [(i, (i + k) % nh) for i in range(nh)])  5.63 us
    all_to_all x1, starting transfers between devices, local(): lax.all_to_all(halves.reshape(n, 1024 // n, 128), ('dev', 'ha'), 0, 0, ti...  4.55 us
    ppermute x3, waiting for transfers between devices, local(): lax.ppermute(blocks[k], 'ha', [(i, (i + k) % nh) for i in range(nh)])  4.35 us
    all_to_all x1, waiting for transfers between devices, local(): lax.all_to_all(halves.reshape(n, 1024 // n, 128), ('dev', 'ha'), 0, 0, ti...  3.97 us
    ppermute x1, starting transfers between devices, diagonal(): return lax.ppermute(block, ('dev', 'ha'), route)  3.79 us
  transfers between devices with their start and end apart: 12, of which 6 were waited for; matrix products, arithmetic and copies ran while one was open for 3% of the time, Pallas kernels for 21%

profile of v4, /device:TPU:0, one launch (start us, length us, event | category | flops | bytes accessed | tf_op | source)
XLA Modules:
  0.0 84.3 jit_solution(6321529789812793159)
XLA Ops:
  0.6 3.2 %collective-permute-start.1 = (bf16[4,8,16,512]{3,2,1,0:T(8,128)(2,1)}, bf16[4,8,16,512]{3,2,1,0:T(8,128)(2,1)}, u32[]{:S(2)}, u32[]{:S(2)}) collective-permute-start(bf16[4,8,16,512]{3,2,1,0:T(8,128)(2,1)} %refs_1_.1), channel_id=1, source_target_pairs={{0,4},{4,8},{8,12},{12,16},{16,20},{20,24},{24,28},{1,5},{5,9},{9,... | collective-permute-start | bytes 1572872 | tf_op jit(solution)/shard_map/ppermute | solution.py:44
  3.8 1.0 %copy_bitcast_fusion = bf16[8,32,512]{2,1,0:T(8,128)(2,1)S(1)} fusion(bf16[4,8,16,512]{3,2,1,0:T(8,128)(2,1)} %refs_1_.1), kind=kLoop, calls=%fused_computation.2 | loop fusion | bytes 524288 | tf_op jit(solution)/shard_map/reshape | solution.py:461
  4.8 4.3 %collective-permute-start = (bf16[8,32,512]{2,1,0:T(8,128)(2,1)S(1)}, bf16[8,32,512]{2,1,0:T(8,128)(2,1)S(1)}, u32[]{:S(2)}, u32[]{:S(2)}) collective-permute-start(bf16[8,32,512]{2,1,0:T(8,128)(2,1)S(1)} %copy_bitcast_fusion), channel_id=1, source_target_pairs={{0,1},{1,2},{2,3},{4,5},{5,6},{6,7},{8,9},{9,10},{10,11},{12,13},{... | collective-permute-start | bytes 786440 | tf_op jit(solution)/shard_map/ppermute | solution.py:44
  9.1 3.8 %collective-permute-start.2 = (bf16[8,32,512]{2,1,0:T(8,128)(2,1)S(1)}, bf16[8,32,512]{2,1,0:T(8,128)(2,1)S(1)}, u32[]{:S(2)}, u32[]{:S(2)}) collective-permute-start(bf16[8,32,512]{2,1,0:T(8,128)(2,1)S(1)} %copy_bitcast_fusion), channel_id=1, source_target_pairs={{0,5},{1,6},{2,7},{4,9},{5,10},{6,11},{8,13},{9,14},{10,15},{12,17... | collective-permute-start | bytes 786440 | tf_op jit(solution)/shard_map/ppermute | solution.py:50
  12.9 0.9 %copy-done = bf16[3,3,3,64,32]{3,4,2,1,0:T(8,128)(2,1)S(1)} copy-done((bf16[3,3,3,64,32]{3,4,2,1,0:T(8,128)(2,1)S(1)}, bf16[3,3,3,64,32]{3,4,2,1,0:T(8,128)(2,1)}, u32[]{:S(2)}) %copy-start) | copy-done | bytes 110616
  13.8 0.8 copy-done.2
  14.7 0.9 %prep.1 = bf16[4,32,1856]{2,1,0:T(8,128)(2,1)} custom-call(bf16[32,8,64]{2,1,0:T(8,128)(2,1)S(1)} %bitcast.34, bf16[27,32,64]{2,1,0:T(8,128)(2,1)S(1)} %bitcast.31), custom_call_target="tpu_custom_call" | custom-call | flops 268435456 | bytes 1048576 | tf_op jit(solution)/shard_map/prep/pallas_call | solution.py:25
  15.6 3.5 %all-to-all-start = ((bf16[4,32,1856]{2,1,0:T(8,128)(2,1)}), bf16[4,32,1856]{2,1,0:T(8,128)(2,1)S(1)}, u32[]{:S(2)}, u32[]{:S(2)}) async-start(bf16[4,32,1856]{2,1,0:T(8,128)(2,1)} %prep.1), calls=%async_computation | async-start | bytes 983040 | tf_op jit(solution)/shard_map/all_to_all | solution.py:469
  19.1 2.3 %collective-permute-done.2.refs_4_ = bf16[8,32,512]{2,1,0:T(8,128)(2,1)S(1)} collective-permute-done((bf16[8,32,512]{2,1,0:T(8,128)(2,1)S(1)}, bf16[8,32,512]{2,1,0:T(8,128)(2,1)S(1)}, u32[]{:S(2)}, u32[]{:S(2)}) %collective-permute-start.2) | collective-permute-done | bytes 262176 | tf_op jit(solution)/shard_map/ppermute | solution.py:50
  21.4 0.7 copy-done.9
  22.1 9.4 %first.1 = (bf16[90112,384]{1,0:T(8,128)(2,1)}, f32[67584,256]{1,0:T(8,128)}) custom-call(bf16[27,4,32]{2,1,0:T(4,128)(2,1)} %bitcast.41, bf16[4,8,16,512]{3,2,1,0:T(8,128)(2,1)} %refs_1_.1, bf16[8,32,512]{2,1,0:T(8,128)(2,1)} %copy-done.8, bf16[4,8,16,512]{3,2,1,0:T(8,128)(2,1)} %collective-permute-done.1.refs_3_, bf16[8,32,512]{2,1,0:T(8,128)(2,1)} %copy-done.9, ...), custom_call_target="tpu_custom_call" | custom-call | flops 8589934592 | bytes 1048576 | tf_op jit(solution)/shard_map/first/pallas_call | solution.py:25
  31.5 1.9 %all-to-all-done = bf16[4,32,1856]{2,1,0:T(8,128)(2,1)S(1)} async-done(((bf16[4,32,1856]{2,1,0:T(8,128)(2,1)}), bf16[4,32,1856]{2,1,0:T(8,128)(2,1)S(1)}, u32[]{:S(2)}, u32[]{:S(2)}) %all-to-all-start) | async-done | bytes 475168 | tf_op jit(solution)/shard_map/all_to_all | solution.py:469
  33.4 1.4 %third.1 = (bf16[128,128]{1,0:T(8,128)(2,1)S(1)}, bf16[256,128]{1,0:T(8,128)(2,1)S(1)}, bf16[384,128]{1,0:T(8,128)(2,1)S(1)}, bf16[32,128]{1,0:T(8,128)(2,1)S(1)...) custom-call(bf16[128,1856]{1,0:T(8,128)(2,1)S(1)} %bitcast.29, ...), custom_call_target="tpu_custom_call" | custom-call | flops 268435456 | bytes 1048576 | tf_op jit(solution)/shard_map/third/pallas_call | solution.py:25
  34.9 1.4 %collective-permute-start.7 = (bf16[256,128]{1,0:T(8,128)(2,1)S(1)}, bf16[256,128]{1,0:T(8,128)(2,1)S(1)}, u32[]{:S(2)}, u32[]{:S(2)}) collective-permute-start(bf16[256,128]{1,0:T(8,128)(2,1)S(1)} %get-tuple-element.29), channel_id=1, source_target_pairs={{1,0},{2,1},{3,2},{5,4},{6,5},{7,6},{9,8},{10,9},{11,10},{13,12},{... | collective-permute-start | bytes 196616 | tf_op jit(solution)/shard_map/ppermute | solution.py:44
  36.4 0.3 copy.20
  36.6 1.4 %third_grad.1 = (bf16[8,128,128]{2,1,0:T(8,128)(2,1)S(1)}, bf16[8,128,128]{2,1,0:T(8,128)(2,1)S(1)}) custom-call(bf16[128,128]{1,0:T(8,128)(2,1)S(1)} %get-tuple-element.26.d3_ref, bf16[90112,384]{1,0:T(8,128)(2,1)} %get-tuple-element.20.park_b), custom_call_target="tpu_custom_call" | custom-call | flops 4294967296 | bytes 1048576 | tf_op jit(solution)/shard_map/third_grad/pallas_call | solution.py:25
  38.3 3.0 %collective-permute-done.7.rz_ref = bf16[256,128]{1,0:T(8,128)(2,1)S(1)} collective-permute-done((bf16[256,128]{1,0:T(8,128)(2,1)S(1)}, bf16[256,128]{1,0:T(8,128)(2,1)S(1)}, u32[]{:S(2)}, u32[]{:S(2)}) %collective-permute-start.7) | collective-permute-done | bytes 65568 | tf_op jit(solution)/shard_map/ppermute | solution.py:44
  41.3 1.3 %collective-permute-start.8 = (bf16[576,128]{1,0:T(8,128)(2,1)S(1)}, bf16[576,128]{1,0:T(8,128)(2,1)S(1)}, u32[]{:S(2)}, u32[]{:S(2)}) collective-permute-start(bf16[576,128]{1,0:T(8,128)(2,1)S(1)} %pad_maximum_fusion.1), channel_id=1, source_target_pairs={{4,0},{8,4},{12,8},{16,12},{20,16},{24,20},{28,24},{5,1},{9,5},{13... | collective-permute-start | bytes 442376 | tf_op jit(solution)/shard_map/ppermute | solution.py:44
  42.6 0.8 add_convert_fusion
  43.3 4.5 %all-to-all-start.1 = ((bf16[32,32,128]{2,1,0:T(8,128)(2,1)}), bf16[32,32,128]{2,1,0:T(8,128)(2,1)S(1)}, u32[]{:S(2)}, u32[]{:S(2)}) async-start(bf16[32,32,128]{2,1,0:T(8,128)(2,1)} %bitcast.10), calls=%async_computation.1 | async-start | bytes 524288 | tf_op jit(solution)/shard_map/all_to_all | solution.py:494
  48.0 6.1 %backward.1 = bf16[512,128]{1,0:T(8,128)(2,1)S(1)} custom-call(bf16[128,768]{1,0:T(8,128)(2,1)S(1)} %copy-done.4, bf16[128,128]{1,0:T(8,128)(2,1)S(1)} %get-tuple-element.26.d3_ref, bf16[256,128]{1,0:T(8,128)(2,1)S(1)} %collective-permute-done.7.rz_ref, bf16[576,128]{1,0:T(8,128)(2,1)S(1)} %collective-permute-done.8.rd_ref, ...), custom_call_target="tpu_custom_call" | custom-call | flops 68719476736 | bytes 1048576 | tf_op jit(solution)/shard_map/backward/pallas_call | solution.py:25
  54.1 4.0 %all-to-all-done.1.g3_ref = bf16[32,32,128]{2,1,0:T(8,128)(2,1)S(1)} async-done(((bf16[32,32,128]{2,1,0:T(8,128)(2,1)}), bf16[32,32,128]{2,1,0:T(8,128)(2,1)S(1)}, u32[]{:S(2)}, u32[]{:S(2)}) %all-to-all-start.1) | async-done | bytes 262176 | tf_op jit(solution)/shard_map/all_to_all | solution.py:494
  58.1 10.9 %all_to_all.20.msg_ref = bf16[32,16,128]{2,1,0:T(8,128)(2,1)S(1)} all-to-all(bf16[32,16,128]{2,1,0:T(8,128)(2,1)S(1)} %bitcast.30), channel_id=1, replica_groups=mesh['dev'=8,'ha'=4] {'dev','ha'}, dimensions={0} | all-to-all | bytes 262144 | tf_op jit(solution)/shard_map/all_to_all | solution.py:514
  69.0 0.8 sum.1
  69.8 2.6 %all-to-all-start.3 = ((bf16[32,32,128]{2,1,0:T(8,128)(2,1)}), bf16[32,32,128]{2,1,0:T(8,128)(2,1)S(1)}, u32[]{:S(2)}, u32[]{:S(2)}) async-start(bf16[32,32,128]{2,1,0:T(8,128)(2,1)} %bitcast.18), calls=%async_computation.3 | async-start | bytes 524288 | tf_op jit(solution)/shard_map/all_to_all | solution.py:517
  72.4 1.7 %collective-permute-start.3 = (bf16[32,128]{1,0:T(8,128)(2,1)S(1)}, bf16[32,128]{1,0:T(8,128)(2,1)S(1)}, u32[]{:S(2)}, u32[]{:S(2)}) collective-permute-start(bf16[32,128]{1,0:T(8,128)(2,1)S(1)} %get-tuple-element.23), channel_id=1, source_target_pairs={{0,1},{1,2},{2,3},{3,0},{4,5},{5,6},{6,7},{7,4},{8,9},{9,10},{10,1... | collective-permute-start | bytes 24584 | tf_op jit(solution)/shard_map/ppermute | solution.py:499
  74.1 2.5 %collective-permute-start.4 = (bf16[32,128]{1,0:T(8,128)(2,1)S(1)}, bf16[32,128]{1,0:T(8,128)(2,1)S(1)}, u32[]{:S(2)}, u32[]{:S(2)}) collective-permute-start(bf16[32,128]{1,0:T(8,128)(2,1)S(1)} %get-tuple-element.24), channel_id=1, source_target_pairs={{0,2},{1,3},{2,0},{3,1},{4,6},{5,7},{6,4},{7,5},{8,10},{9,11},{10,... | collective-permute-start | bytes 24584 | tf_op jit(solution)/shard_map/ppermute | solution.py:499
  76.6 1.4 %collective-permute-start.5 = (bf16[32,128]{1,0:T(8,128)(2,1)S(1)}, bf16[32,128]{1,0:T(8,128)(2,1)S(1)}, u32[]{:S(2)}, u32[]{:S(2)}) collective-permute-start(bf16[32,128]{1,0:T(8,128)(2,1)S(1)} %get-tuple-element.25), channel_id=1, source_target_pairs={{0,3},{1,0},{2,1},{3,2},{4,7},{5,4},{6,5},{7,6},{8,11},{9,8},{10,9... | collective-permute-start | bytes 24584 | tf_op jit(solution)/shard_map/ppermute | solution.py:499
  78.0 3.6 %collective-permute-done.3.refs_1_ = bf16[32,128]{1,0:T(8,128)(2,1)S(1)} collective-permute-done((bf16[32,128]{1,0:T(8,128)(2,1)S(1)}, bf16[32,128]{1,0:T(8,128)(2,1)S(1)}, u32[]{:S(2)}, u32[]{:S(2)}) %collective-permute-start.3) | collective-permute-done | bytes 8224 | tf_op jit(solution)/shard_map/ppermute | solution.py:499
  81.7 0.7 collective-permute-done.4.refs_2_
  82.5 0.7 copy.19
  83.2 1.1 %unpack.1 = (f32[27,4,32]{2,1,0:T(4,128)}, f32[2,27,16,64]{3,2,1,0:T(8,128)}, f32[27,32,64]{2,1,0:T(8,128)}) custom-call(bf16[32,32,128]{2,1,0:T(8,128)(2,1)S(1)} %all-to-all-done.3.total_ref), custom_call_target="tpu_custom_call" | custom-call | flops 268435456 | bytes 1048576 | tf_op jit(solution)/shard_map/unpack/pallas_call | solution.py:25
  (31 shorter events, 0.4 us)
Async XLA Ops:
  0.6 21.5 %collective-permute-start.1 = (bf16[4,8,16,512]{3,2,1,0:T(8,128)(2,1)}, bf16[4,8,16,512]{3,2,1,0:T(8,128)(2,1)}, u32[]{:S(2)}, u32[]{:S(2)}) collective-permute-start(bf16[4,8,16,512]{3,2,1,0:T(8,128)(2,1)} %refs_1_.1), channel_id=1, source_target_pairs={{0,4},{4,8},{8,12},{12,16},{16,20},{20,24},{24,28},{1,5},{5,9},{9,... | collective-permute-start | bytes 1572872 | tf_op jit(solution)/shard_map/ppermute | solution.py:44
  4.8 14.3 %collective-permute-start = (bf16[8,32,512]{2,1,0:T(8,128)(2,1)S(1)}, bf16[8,32,512]{2,1,0:T(8,128)(2,1)S(1)}, u32[]{:S(2)}, u32[]{:S(2)}) collective-permute-start(bf16[8,32,512]{2,1,0:T(8,128)(2,1)S(1)} %copy_bitcast_fusion), channel_id=1, source_target_pairs={{0,1},{1,2},{2,3},{4,5},{5,6},{6,7},{8,9},{9,10},{10,11},{12,13},{... | collective-permute-start | bytes 786440 | tf_op jit(solution)/shard_map/ppermute | solution.py:44
  9.1 12.3 %collective-permute-start.2 = (bf16[8,32,512]{2,1,0:T(8,128)(2,1)S(1)}, bf16[8,32,512]{2,1,0:T(8,128)(2,1)S(1)}, u32[]{:S(2)}, u32[]{:S(2)}) collective-permute-start(bf16[8,32,512]{2,1,0:T(8,128)(2,1)S(1)} %copy_bitcast_fusion), channel_id=1, source_target_pairs={{0,5},{1,6},{2,7},{4,9},{5,10},{6,11},{8,13},{9,14},{10,15},{12,17... | collective-permute-start | bytes 786440 | tf_op jit(solution)/shard_map/ppermute | solution.py:50
  12.9 0.9 %copy-start = (bf16[3,3,3,64,32]{3,4,2,1,0:T(8,128)(2,1)S(1)}, bf16[3,3,3,64,32]{3,4,2,1,0:T(8,128)(2,1)}, u32[]{:S(2)}) copy-start(bf16[3,3,3,64,32]{3,4,2,1,0:T(8,128)(2,1)} %param.14) | copy-start | bytes 331780
  13.8 0.8 copy-start.2
  15.6 17.8 %all-to-all-start = ((bf16[4,32,1856]{2,1,0:T(8,128)(2,1)}), bf16[4,32,1856]{2,1,0:T(8,128)(2,1)S(1)}, u32[]{:S(2)}, u32[]{:S(2)}) async-start(bf16[4,32,1856]{2,1,0:T(8,128)(2,1)} %prep.1), calls=%async_computation | async-start | bytes 983040 | tf_op jit(solution)/shard_map/all_to_all | solution.py:469
  19.1 3.0 %copy-start.8 = (bf16[8,32,512]{2,1,0:T(8,128)(2,1)}, bf16[8,32,512]{2,1,0:T(8,128)(2,1)S(1)}, u32[]{:S(2)}) copy-start(bf16[8,32,512]{2,1,0:T(8,128)(2,1)S(1)} %collective-permute-done.refs_2_) | copy-start | bytes 786436
  21.4 0.7 copy-start.9
  34.9 13.0 %copy-start.1 = (bf16[3,3,3,32,64]{4,3,2,1,0:T(8,128)(2,1)S(1)}, bf16[3,3,3,32,64]{4,3,2,1,0:T(8,128)(2,1)}, u32[]{:S(2)}) copy-start(bf16[3,3,3,32,64]{4,3,2,1,0:T(8,128)(2,1)} %param.13) | copy-start | bytes 331780
  34.9 13.0 %copy-start.3 = (bf16[3,288,256]{2,1,0:T(8,128)(2,1)S(1)}, bf16[3,288,256]{2,1,0:T(8,128)(2,1)}, u32[]{:S(2)}) copy-start(bf16[3,288,256]{2,1,0:T(8,128)(2,1)} %constant.14.clone.mask_ref) | copy-start | bytes 1327108
  34.9 13.0 %copy-start.4 = (bf16[128,768]{1,0:T(8,128)(2,1)S(1)}, bf16[128,768]{1,0:T(8,128)(2,1)}, u32[]{:S(2)}) copy-start(bf16[128,768]{1,0:T(8,128)(2,1)} %constant.17.clone.spread_ref) | copy-start | bytes 589828
  34.9 13.0 %copy-start.5 = (bf16[256,32]{1,0:T(8,128)(2,1)S(1)}, bf16[256,32]{1,0:T(8,128)(2,1)}, u32[]{:S(2)}) copy-start(bf16[256,32]{1,0:T(8,128)(2,1)} %constant.12.clone.so_ref) | copy-start | bytes 49156
  34.9 13.0 %copy-start.6 = (bf16[128,128]{1,0:T(8,128)(2,1)S(1)}, bf16[128,128]{1,0:T(8,128)(2,1)}, u32[]{:S(2)}) copy-start(bf16[128,128]{1,0:T(8,128)(2,1)} %constant.15.clone.refs_5_.later_ref) | copy-start | bytes 98308
  34.9 13.0 %copy-start.7 = (bf16[16,288]{1,0:T(8,128)(2,1)S(1)}, bf16[16,288]{1,0:T(8,128)(2,1)}, u32[]{:S(2)}) copy-start(bf16[16,288]{1,0:T(8,128)(2,1)} %constant.13.clone.sam_ref) | copy-start | bytes 27652
  34.9 6.3 %collective-permute-start.7 = (bf16[256,128]{1,0:T(8,128)(2,1)S(1)}, bf16[256,128]{1,0:T(8,128)(2,1)S(1)}, u32[]{:S(2)}, u32[]{:S(2)}) collective-permute-start(bf16[256,128]{1,0:T(8,128)(2,1)S(1)} %get-tuple-element.29), channel_id=1, source_target_pairs={{1,0},{2,1},{3,2},{5,4},{6,5},{7,6},{9,8},{10,9},{11,10},{13,12},{... | collective-permute-start | bytes 196616 | tf_op jit(solution)/shard_map/ppermute | solution.py:44
  38.1 4.5 %collective-permute-start.6 = (bf16[8,128,128]{2,1,0:T(8,128)(2,1)S(1)}, bf16[8,128,128]{2,1,0:T(8,128)(2,1)S(1)}, u32[]{:S(2)}, u32[]{:S(2)}) collective-permute-start(bf16[8,128,128]{2,1,0:T(8,128)(2,1)S(1)} %get-tuple-element.28), channel_id=1, source_target_pairs={{0,4},{4,0},{8,12},{12,8},{16,20},{20,16},{24,28},{28,24},{1,5},{5... | collective-permute-start | bytes 786440 | tf_op jit(solution)/shard_map/ppermute | solution.py:492
  41.3 6.6 %collective-permute-start.8 = (bf16[576,128]{1,0:T(8,128)(2,1)S(1)}, bf16[576,128]{1,0:T(8,128)(2,1)S(1)}, u32[]{:S(2)}, u32[]{:S(2)}) collective-permute-start(bf16[576,128]{1,0:T(8,128)(2,1)S(1)} %pad_maximum_fusion.1), channel_id=1, source_target_pairs={{4,0},{8,4},{12,8},{16,12},{20,16},{24,20},{28,24},{5,1},{9,5},{13... | collective-permute-start | bytes 442376 | tf_op jit(solution)/shard_map/ppermute | solution.py:44
  43.3 14.8 %all-to-all-start.1 = ((bf16[32,32,128]{2,1,0:T(8,128)(2,1)}), bf16[32,32,128]{2,1,0:T(8,128)(2,1)S(1)}, u32[]{:S(2)}, u32[]{:S(2)}) async-start(bf16[32,32,128]{2,1,0:T(8,128)(2,1)} %bitcast.10), calls=%async_computation.1 | async-start | bytes 524288 | tf_op jit(solution)/shard_map/all_to_all | solution.py:494
  69.8 13.4 %all-to-all-start.3 = ((bf16[32,32,128]{2,1,0:T(8,128)(2,1)}), bf16[32,32,128]{2,1,0:T(8,128)(2,1)S(1)}, u32[]{:S(2)}, u32[]{:S(2)}) async-start(bf16[32,32,128]{2,1,0:T(8,128)(2,1)} %bitcast.18), calls=%async_computation.3 | async-start | bytes 524288 | tf_op jit(solution)/shard_map/all_to_all | solution.py:517
  72.4 9.3 %collective-permute-start.3 = (bf16[32,128]{1,0:T(8,128)(2,1)S(1)}, bf16[32,128]{1,0:T(8,128)(2,1)S(1)}, u32[]{:S(2)}, u32[]{:S(2)}) collective-permute-start(bf16[32,128]{1,0:T(8,128)(2,1)S(1)} %get-tuple-element.23), channel_id=1, source_target_pairs={{0,1},{1,2},{2,3},{3,0},{4,5},{5,6},{6,7},{7,4},{8,9},{9,10},{10,1... | collective-permute-start | bytes 24584 | tf_op jit(solution)/shard_map/ppermute | solution.py:499
  74.1 8.2 %collective-permute-start.4 = (bf16[32,128]{1,0:T(8,128)(2,1)S(1)}, bf16[32,128]{1,0:T(8,128)(2,1)S(1)}, u32[]{:S(2)}, u32[]{:S(2)}) collective-permute-start(bf16[32,128]{1,0:T(8,128)(2,1)S(1)} %get-tuple-element.24), channel_id=1, source_target_pairs={{0,2},{1,3},{2,0},{3,1},{4,6},{5,7},{6,4},{7,5},{8,10},{9,11},{10,... | collective-permute-start | bytes 24584 | tf_op jit(solution)/shard_map/ppermute | solution.py:499
  76.6 5.7 %collective-permute-start.5 = (bf16[32,128]{1,0:T(8,128)(2,1)S(1)}, bf16[32,128]{1,0:T(8,128)(2,1)S(1)}, u32[]{:S(2)}, u32[]{:S(2)}) collective-permute-start(bf16[32,128]{1,0:T(8,128)(2,1)S(1)} %get-tuple-element.25), channel_id=1, source_target_pairs={{0,3},{1,0},{2,1},{3,2},{4,7},{5,4},{6,5},{7,6},{8,11},{9,8},{10,9... | collective-permute-start | bytes 24584 | tf_op jit(solution)/shard_map/ppermute | solution.py:499
